TPU v7x, 32 devices: a whole 2x2x4 slice. The times are simulated.
32 devices in a mesh: branch: 2 (over x), mp: 2 (over y), dp: 8 (over z, core).
Axes of the slice: x: 2, y: 2, z: 4, core: 2. Of those that a mesh axis runs over, the one named last changes fastest.
Arguments:
- block_input: bfloat16 [16, 512, 2048], P('dp'), may hold values from -6 to 6
- cotangent: bfloat16 [16, 512, 2048], P('dp', None, ('branch', 'mp')), may hold values from -6 to 6
- segments: int32 [16, 512], P('dp'), may hold values from 0 to 3, never falling along the last dimension, each value on 1 to 256 neighbouring positions
- attend_gain: float32 [2048], replicated, may hold values from 0.5 to 1.5
- attend_shift: float32 [2048], replicated, may hold values from -0.8 to 0.8
- joined_weight: bfloat16 [2048, 6144], P('dp', 'mp'), may hold values from -0.125 to 0.125
- joined_bias: float32 [6144], replicated, may hold values from -0.5 to 0.5
- dense_weight: bfloat16 [2048, 2048], P(('mp', 'dp')), may hold values from -0.5 to 0.5
- dense_bias: float32 [2048], replicated, may hold values from -1.2 to 1.2
- expand_gain: float32 [2048], replicated, may hold values from 0.5 to 1.5
- expand_shift: float32 [2048], replicated, may hold values from -0.8 to 0.8
- up_weight: bfloat16 [2048, 8192], P('dp', 'mp'), may hold values from -0.125 to 0.125
- up_bias: float32 [8192], replicated, may hold values from -1.2 to 1.2
- down_weight: bfloat16 [8192, 2048], P(('mp', 'dp')), may hold values from -0.0625 to 0.0625
- down_bias: float32 [2048], replicated, may hold values from -1.2 to 1.2
Outputs:
- block_output: bfloat16 [16, 512, 2048], P('dp', None, ('branch', 'mp'))
- input_gradient: bfloat16 [16, 512, 2048], P('dp', None, ('branch', 'mp'))
- attend_gain_gradient: float32 [2048], replicated
- attend_shift_gradient: float32 [2048], replicated
- joined_weight_gradient: float32 [2048, 6144], P(('branch', 'dp'), 'mp')
- joined_bias_gradient: float32 [6144], replicated
- dense_weight_gradient: float32 [2048, 2048], P('mp', ('branch', 'dp'))
- dense_bias_gradient: float32 [2048], replicated
- expand_gain_gradient: float32 [2048], replicated
- expand_shift_gradient: float32 [2048], replicated
- up_weight_gradient: float32 [2048, 8192], P(('branch', 'dp'), 'mp')
- up_bias_gradient: float32 [8192], replicated
- down_weight_gradient: float32 [8192, 2048], P('mp', ('branch', 'dp'))
- down_bias_gradient: float32 [2048], replicated
Inputs may be any that keep to these rules, and one draw needn't show every extreme that they name: `segments`: along a row the ids never fall and each id holds 1 to 256 of the row's tokens.
All inputs are finite; a program needn't handle non-finite values.
Results may differ from a plain program's by a relative error of at most 0.0092.
Values may be sent and summed in bfloat16 or wider, within the bound.
No kernel may reach another device: no remote copies, remote signals or barrier semaphores. Data moves between devices by JAX's collectives and lax.ppermute only.
A program may use at most 576 MiB of HBM per device.

v0:
```python
import functools
import math

import jax
import jax.numpy as jnp
from jax import lax
from jax.experimental import pallas as pl
from jax.experimental.pallas import tpu as pltpu
from jax.sharding import Mesh, PartitionSpec as P

HEAD = 256
ROT = 64
LANES = 128
NEGATIVE = -1e30
VMEM_BYTES = 56 * 1024 * 1024
F32 = jnp.float32
BF16 = jnp.bfloat16


def rotary_tables(segment_rows):
    length = segment_rows.shape[1]
    before = jnp.sum(
        (segment_rows[:, None, :] < segment_rows[:, :, None]).astype(jnp.int32), axis=2
    )
    places = (jnp.arange(length, dtype=jnp.int32)[None] - before).astype(F32)
    frequency = 10000.0 ** (-jnp.arange(0, ROT, 2).astype(F32) / ROT)
    angles = (places[:, :, None] * frequency).reshape(-1, ROT // 2)
    cosine, sine = jnp.cos(angles), jnp.sin(angles)
    none = jnp.zeros_like(sine)
    rest = jnp.zeros((angles.shape[0], LANES - ROT), F32)
    return (
        jnp.concatenate([cosine, cosine, rest + 1.0], axis=1),
        jnp.concatenate([-sine, none, rest], axis=1),
        jnp.concatenate([none, sine, rest], axis=1),
    )


def rotate(values, self_factor, right_factor, left_factor):
    half = ROT // 2
    front = values[:, :LANES]
    turned = (
        front * self_factor
        + pltpu.roll(front, LANES - half, 1) * right_factor
        + pltpu.roll(front, half, 1) * left_factor
    )
    return jnp.concatenate([turned, values[:, LANES:]], axis=1)


def dot(left, right, left_dim, right_dim):
    return lax.dot_general(
        left, right, (((left_dim,), (right_dim,)), ((), ())), preferred_element_type=F32
    )


def whole(shape):
    return pl.BlockSpec(shape, lambda i: (0,) * len(shape), pipeline_mode=pl.Buffered(1))


def tile(rows, columns):
    return pl.BlockSpec((rows, columns), lambda i: (i, 0))


def run(body, steps, ins, outs, args, flops, transcendentals=0):
    scratch = []
    if any(isinstance(arg, Line) for arg in args):
        body, ins, args, scratch = put_together(body, ins, args)
    shapes = [jax.ShapeDtypeStruct(shape, dtype) for _, shape, dtype in outs]
    moved = sum(a.size * a.dtype.itemsize for a in list(args) + shapes)
    return pl.pallas_call(
        body,
        grid=(steps,),
        in_specs=ins,
        out_specs=[spec for spec, _, _ in outs],
        out_shape=shapes,
        scratch_shapes=scratch,
        cost_estimate=pl.CostEstimate(
            flops=flops // 64, bytes_accessed=moved // 64, transcendentals=transcendentals // 64
        ),
        compiler_params=pltpu.CompilerParams(vmem_limit_bytes=VMEM_BYTES),
    )(*args)


def put_together(body, ins, args):
    new_ins, new_args, places, scratch = [], [], [], []
    for spec, arg in zip(ins, args):
        if not isinstance(arg, Line):
            new_ins.append(spec)
            new_args.append(arg)
            places.append(None)
        elif arg.full is not None:
            new_ins.append(spec)
            new_args.append(arg.full)
            places.append(None)
        else:
            slots = arg.slots()
            rows, columns = slots[0].shape
            new_ins += [pl.BlockSpec(memory_space=pl.ANY)] * len(slots)
            new_args += slots
            places.append((len(slots), rows, arg.count))
            scratch += [
                pltpu.VMEM((arg.count * rows, columns), slots[0].dtype),
                pltpu.SemaphoreType.DMA((arg.count,)),
            ]
            index = arg.index
    if not scratch:
        return body, new_ins, new_args, []

    def whole_body(index_ref, *refs):
        kept, held = refs[: len(refs) - len(scratch)], refs[len(refs) - len(scratch) :]
        inner, lines, at = [], [], 0
        for place in places:
            if place is None:
                inner.append(kept[at])
                at += 1
            else:
                full_ref, sems = held[2 * len(lines) : 2 * len(lines) + 2]
                lines.append((kept[at : at + place[0]], full_ref, sems, place))
                inner.append(full_ref)
                at += place[0]

        @pl.when(pl.program_id(0) == 0)
        def _():
            for blocks, full_ref, sems, (_, rows, count) in lines:
                for j in range(count):
                    for k, block in enumerate(blocks):

                        @pl.when(count - 1 - index_ref[0] + j == k)
                        def _():
                            pltpu.make_async_copy(
                                block, full_ref.at[pl.ds(j * rows, rows)], sems.at[j]
                            ).start()

            for blocks, full_ref, sems, (_, rows, count) in lines:
                for j in range(count):
                    pltpu.make_async_copy(
                        blocks[0], full_ref.at[pl.ds(j * rows, rows)], sems.at[j]
                    ).wait()

        body(*inner, *kept[at:])

    return (
        whole_body,
        [pl.BlockSpec(memory_space=pltpu.SMEM)] + new_ins,
        [index.reshape(1)] + new_args,
        scratch,
    )


def statistics(x):
    mean = jnp.mean(x, axis=-1, keepdims=True)
    center = x - mean
    inverse = lax.rsqrt(jnp.mean(center * center, axis=-1, keepdims=True) + 1e-05)
    return center * inverse, mean, inverse


def either(steps, mine_ref, other_ref):
    return jnp.where(pl.program_id(0) < steps, mine_ref[...], other_ref[...])


def halves(rows, columns, steps):
    return [
        pl.BlockSpec((rows, columns), lambda i: (jnp.minimum(i, steps - 1), 0)),
        pl.BlockSpec((rows, columns), lambda i: (jnp.maximum(i - steps, 0), 0)),
    ]


def norm_body(steps, mine_ref, other_ref, gain_a, shift_a, gain_e, shift_e, normed_ref, expanded_ref, stats_ref):
    hat, mean, inverse = statistics(either(steps, mine_ref, other_ref).astype(F32))
    lane = lax.broadcasted_iota(jnp.int32, stats_ref.shape, 1)
    stats_ref[...] = jnp.where(lane == 0, mean, inverse)
    normed_ref[...] = (hat * gain_a[...] + shift_a[...]).astype(BF16)
    expanded_ref[...] = (hat * gain_e[...] + shift_e[...]).astype(BF16)


def gather_body(steps, starts_ref, *refs):
    pieces, out_ref = refs[:-1], refs[-1]
    span = pieces[0].shape[1]
    for k in range(len(pieces) // 2):
        columns = pl.ds(pl.multiple_of(starts_ref[k], span), span)
        out_ref[:, columns] = either(steps, pieces[2 * k], pieces[2 * k + 1])


def accumulate(ref, value):
    @pl.when(pl.program_id(0) == 0)
    def _():
        ref[...] = value

    @pl.when(pl.program_id(0) != 0)
    def _():
        ref[...] += value


def attention_body(
    normed_ref, joined_ref, bias_ref, self_ref, right_ref, left_ref, column_ref, row_ref, g_ref, dense_ref,
    mixed_ref, grad_ref, bias_grad_ref,
):
    length = normed_ref.shape[0]
    scale = 1.0 / math.sqrt(HEAD)
    factors = self_ref[...], right_ref[...], left_ref[...]
    raw = dot(normed_ref[...], joined_ref[...], 1, 0) + bias_ref[...]
    queries = (rotate(raw[:, :HEAD], *factors) * scale).astype(BF16)
    keyset = rotate(raw[:, HEAD : 2 * HEAD], *factors).astype(BF16)
    valueset = raw[:, 2 * HEAD :].astype(BF16)
    query_index = lax.broadcasted_iota(jnp.int32, (length, length), 0)
    key_index = lax.broadcasted_iota(jnp.int32, (length, length), 1)
    allowed = (column_ref[0] == row_ref[0]) & (key_index <= query_index)
    scores = jnp.where(allowed, dot(queries, keyset, 1, 1), NEGATIVE)
    shifted = jnp.exp(scores - jnp.max(scores, axis=-1, keepdims=True))
    probs = shifted / jnp.sum(shifted, axis=-1, keepdims=True)
    low = probs.astype(BF16)
    mixed_ref[...] = dot(low, valueset, 1, 0).astype(BF16)
    mixed_grad = dot(g_ref[...], dense_ref[...], 1, 1).astype(BF16)
    probs_grad = dot(mixed_grad, valueset, 1, 1)
    value_grad = dot(low, mixed_grad, 0, 0)
    inner = jnp.sum(probs_grad * probs, axis=-1, keepdims=True)
    score_grad = (probs * (probs_grad - inner)).astype(BF16)
    query_grad = rotate(dot(score_grad, keyset, 1, 0) * scale, *back_factors(factors))
    key_grad = rotate(dot(score_grad, queries, 0, 0), *back_factors(factors))
    joined_grad = jnp.concatenate([query_grad, key_grad, value_grad], axis=1).astype(BF16)
    grad_ref[...] = joined_grad
    accumulate(bias_grad_ref, jnp.sum(joined_grad.astype(F32), axis=0, keepdims=True))


def back_factors(factors):
    return factors[0], -factors[1], -factors[2]


def hidden_body(expanded_ref, up_ref, bias_ref, activated_ref, slope_ref):
    block = up_ref.shape[1] // 4
    for k in range(4):
        columns = pl.ds(k * block, block)
        hidden = dot(expanded_ref[...], up_ref[:, columns], 1, 0) + bias_ref[:, columns]
        below = 0.5 * (1.0 + lax.erf(hidden * math.sqrt(0.5)))
        density = jnp.exp(hidden * hidden * -0.5) * (1.0 / math.sqrt(2.0 * math.pi))
        activated_ref[:, columns] = (hidden * below).astype(BF16)
        slope_ref[:, columns] = (below + hidden * density).astype(BF16)


def terms_body(*refs):
    out_ref, start = refs[-1], 0
    for left_ref, right_ref in zip(refs[:-1:2], refs[1:-1:2]):
        stop = start + right_ref.shape[1]
        term = dot(left_ref[...], right_ref[...], 0, 0).astype(BF16)
        out_ref[:, :, :, start:stop] = term.reshape(*out_ref.shape[:3], stop - start)
        start = stop


def hidden_grad_body(g_ref, down_ref, slope_ref, grad_ref, bias_grad_ref):
    grad = dot(g_ref[...], down_ref[...], 1, 1) * slope_ref[...].astype(F32)
    grad = grad.astype(BF16)
    grad_ref[...] = grad
    accumulate(bias_grad_ref, jnp.sum(grad.astype(F32), axis=0, keepdims=True))


def store_blocks(out_ref, values, got_refs):
    blocks, span = out_ref.shape[1], out_ref.shape[3]
    for k in range(blocks):
        block = values[:, k * span : (k + 1) * span]
        for got_ref in got_refs:
            block = block + got_ref[0, k].astype(F32)
        out_ref[0, k] = block.astype(BF16)


def forward_body(mixed_ref, dense_ref, active_ref, down_ref, *refs):
    total = dot(mixed_ref[...], dense_ref[...], 1, 0)
    total += dot(active_ref[...], down_ref[...], 1, 0)
    store_blocks(refs[-1], total, refs[:-1])


def input_body(
    x_ref, stats_ref, joined_grad_ref, joined_ref, hidden_grad_ref, up_ref, gain_a, gain_e, *refs
):
    got_refs, (out_ref, sums_ref) = refs[:-2], refs[-2:]
    normed_grad = dot(joined_grad_ref[...], joined_ref[...], 1, 1)
    expanded_grad = dot(hidden_grad_ref[...], up_ref[...], 1, 1)
    mean, inverse = stats_ref[:, 0:1], stats_ref[:, 1:2]
    hat = (x_ref[...].astype(F32) - mean) * inverse
    weighted = normed_grad * gain_a[...] + expanded_grad * gain_e[...]
    weighted_mean = jnp.mean(weighted, axis=-1, keepdims=True)
    along = jnp.mean(weighted * hat, axis=-1, keepdims=True)
    store_blocks(out_ref, inverse * (weighted - weighted_mean - hat * along), got_refs)

    def down(values):
        return jnp.sum(values, axis=0, keepdims=True)

    sums = jnp.concatenate(
        [down(normed_grad * hat), down(normed_grad), down(expanded_grad * hat), down(expanded_grad)]
    )
    accumulate(sums_ref, sums)


def place_body(layouts, pieces_ref, *outs):
    for device in range(pieces_ref.shape[0]):
        for start, size, target, where, turned in layouts:
            offset = where(device) * size
            values = pieces_ref[device, :, start : start + size].astype(F32)
            if turned:
                outs[target][offset : offset + size, :] = values.T
            else:
                outs[target][:, offset : offset + size] = values


def pick(array, index, axis):
    return lax.dynamic_index_in_dim(array, index, axis, keepdims=False)


def add_low(left, right):
    return (left.astype(F32) + right.astype(F32)).astype(BF16)


SWAP = [(0, 1), (1, 0)]


class Chain:
    def __init__(self, view, index, count):
        self.view, self.index, self.count, self.step = view, index, count, 0
        self.held = self.flight = ()
        self.out = []

    def term(self, share):
        return pick(self.view, jnp.clip(share, 0, self.count - 1), 0)

    def prepare(self):
        if self.step == self.count - 1:
            return
        self.step += 1
        step, count = self.step, self.count
        self.out = [self.term(self.index + count - step), self.term(self.index - count + step)]
        if self.held:
            self.out = [add_low(one, two) for one, two in zip(self.out, self.held)]

    def send(self):
        if not self.out:
            self.prepare()
        if not self.out:
            return
        step, count = self.step, self.count
        self.flight = (
            lax.ppermute(self.out[0], "z", [(i, i + 1) for i in range(step)]),
            lax.ppermute(self.out[1], "z", [(count - 1 - i, count - 2 - i) for i in range(step)]),
        )
        self.out = []

    def land(self, values):
        if values:
            self.held, self.flight = values, ()

    def total(self):
        own = self.term(self.index).astype(F32)
        return (own + self.held[0].astype(F32) + self.held[1].astype(F32)).astype(BF16)


class Line:
    def __init__(self, piece, index, count):
        self.index, self.count, self.step, self.flight = index, count, 0, ()
        self.from_left, self.from_right, self.own, self.full = [], [], piece, None
        if count > 4:
            self.full = lax.all_gather(piece, "z", axis=0, tiled=True)

    def send(self):
        if self.full is not None or self.step == self.count - 1:
            return
        step, count = self.step, self.count
        right, left = (self.from_left[-1], self.from_right[-1]) if step else (self.own, self.own)
        self.flight = (
            lax.ppermute(right, "z", [(i, i + 1) for i in range(step, count - 1)]),
            lax.ppermute(left, "z", [(i + 1, i) for i in range(count - 1 - step)]),
        )
        self.step += 1

    def land(self, values):
        if values:
            self.from_left.append(values[0])
            self.from_right.append(values[1])
            self.flight = ()

    def slots(self):
        return [*self.from_left[::-1], self.own, *self.from_right]


fence = lax.optimization_barrier


def solution(mesh):
    branches, models, datas = (mesh.shape[name] for name in ("branch", "mp", "dp"))
    cores = 2
    chips = datas // cores
    fine = Mesh(
        mesh.devices.reshape(branches, models, chips, cores), ("branch", "mp", "z", "core")
    )

    def on_device(
        block_input,
        cotangent,
        segments,
        attend_gain,
        attend_shift,
        joined_weight,
        joined_bias,
        dense_weight,
        dense_bias,
        expand_gain,
        expand_shift,
        up_weight,
        up_bias,
        down_weight,
        down_bias,
    ):
        rows, length, width = block_input.shape
        b, m, z, c = (lax.axis_index(name) for name in ("branch", "mp", "z", "core"))
        tokens = rows * length
        span = width // (branches * models)
        column_start = (b * models + m) * span
        heads = branches * cores
        head_columns = joined_weight.shape[1] // heads
        hidden_columns = up_weight.shape[1]
        part = down_weight.shape[0] // branches
        units = chips * part
        head_slot = b * cores + c
        row_share = width // (branches * datas)

        def partner(array, **flips):
            names = tuple(name for name, flip in flips.items() if flip)
            if not names:
                return array
            count = 2 ** len(names)
            return lax.ppermute(array, names, [(i, count - 1 - i) for i in range(count)])

        def swap_core(array):
            return partner(array, core=1)

        def in_core_order(mine, other):
            return jnp.where(c == 0, jnp.concatenate([mine, other]), jnp.concatenate([other, mine]))

        def columns_of(array, start, size):
            return lax.dynamic_slice_in_dim(array, start, size, array.ndim - 1)

        def unit_columns(array, core):
            return jnp.concatenate(
                [
                    columns_of(array, ((k * cores + core) * branches + b) * part, part)
                    for k in range(chips)
                ],
                axis=-1,
            )

        def gather(piece):
            return lax.all_gather(piece, "z", axis=0, tiled=True)

        x_own = block_input.reshape(tokens, width)
        g_piece = cotangent.reshape(tokens, span)
        joined_piece = in_core_order(
            columns_of(joined_weight, head_slot * head_columns, head_columns),
            swap_core(columns_of(joined_weight, (b * cores + 1 - c) * head_columns, head_columns)),
        )
        flips = [(db, dm) for db in range(2) for dm in range(2)]
        g_mine = [partner(g_piece, branch=db, mp=dm) for db, dm in flips]
        x_other = swap_core(x_own)
        segment_rows = jnp.concatenate([segments, swap_core(segments)])
        joined_piece, dense_weight = fence((joined_piece, dense_weight))
        spread_dense = chips == heads and HEAD == cores * dense_weight.shape[0]
        if spread_dense:
            few = HEAD // chips
            per_core = chips // cores
            dense_piece = 0
            for j in range(per_core):
                moves = [
                    (
                        (one * chips + one * cores + to) * cores + at,
                        (one * chips + at * per_core + j) * cores + to,
                    )
                    for one in range(branches)
                    for to in range(cores)
                    for at in range(cores)
                ]
                dense_piece = dense_piece + lax.ppermute(
                    dense_weight[j * few : (j + 1) * few], ("branch", "z", "core"), moves
                )
        else:
            dense_piece = dense_weight

        joined_bias_here = columns_of(joined_bias, (m * heads + head_slot) * head_columns, head_columns)
        up_bias_here = unit_columns(columns_of(up_bias, m * hidden_columns, hidden_columns), c)
        down_piece = lax.dynamic_slice_in_dim(down_weight, b * part, part, 0)

        def flat(vector):
            return vector.reshape(1, -1)

        all_tokens = 2 * tokens
        gains = flat(attend_gain), flat(expand_gain)
        small_tile = min(256, length)
        half_steps = tokens // small_tile
        joined_full = gather(joined_piece)
        x_other, joined_piece, up_weight, dense_piece = fence(
            (x_other, joined_piece, up_weight, dense_piece)
        )
        if spread_dense:
            dense_full = gather(dense_piece)
        else:
            dense_full = lax.all_gather(dense_piece, ("z", "core"), axis=0, tiled=True)
            dense_full = lax.dynamic_slice_in_dim(dense_full, head_slot * HEAD, HEAD, 0)
        up_piece = in_core_order(unit_columns(up_weight, c), swap_core(unit_columns(up_weight, 1 - c)))
        normed, expanded, stats = run(
            functools.partial(norm_body, half_steps),
            2 * half_steps,
            halves(small_tile, width, half_steps) + [whole((1, width))] * 4,
            [(tile(small_tile, width), (all_tokens, width), BF16)] * 2
            + [(tile(small_tile, LANES), (all_tokens, LANES), F32)],
            (x_own, x_other, gains[0], flat(attend_shift), gains[1], flat(expand_shift)),
            20 * all_tokens * width,
        )
        rotary = rotary_tables(segment_rows)
        normed, expanded, rotary, g_mine, up_piece, down_piece = fence(
            (normed, expanded, rotary, g_mine, up_piece, down_piece)
        )
        up_line = Line(up_piece, z, chips)
        up_line.send()
        g_other = [swap_core(piece) for piece in g_mine]
        starts = jnp.stack([((b ^ db) * models + (m ^ dm)) * span for db, dm in flips])
        (g,) = run(
            functools.partial(gather_body, half_steps),
            2 * half_steps,
            [pl.BlockSpec(memory_space=pltpu.SMEM)]
            + [spec for _ in flips for spec in halves(small_tile, span, half_steps)],
            [(tile(small_tile, width), (all_tokens, width), BF16)],
            (starts, *[piece for pair in zip(g_mine, g_other) for piece in pair]),
            all_tokens * width,
        )
        up_line.flight, g, down_piece, joined_full, dense_full = fence(
            (up_line.flight, g, down_piece, joined_full, dense_full)
        )
        up_line.land(up_line.flight)
        up_line.send()

        all_rows = 2 * rows
        mixed, joined_grad, joined_bias_grad = run(
            attention_body,
            all_rows,
            [
                tile(length, width),
                whole((width, head_columns)),
                whole((1, head_columns)),
                tile(length, LANES),
                tile(length, LANES),
                tile(length, LANES),
                pl.BlockSpec((1, length, 1), lambda i: (i, 0, 0)),
                pl.BlockSpec((1, 1, length), lambda i: (i, 0, 0)),
                tile(length, width),
                whole((HEAD, width)),
            ],
            [
                (tile(length, HEAD), (all_tokens, HEAD), BF16),
                (tile(length, head_columns), (all_tokens, head_columns), BF16),
                (whole((1, head_columns)), (1, head_columns), F32),
            ],
            (
                normed,
                joined_full,
                flat(joined_bias_here),
                *rotary,
                segment_rows[:, :, None],
                segment_rows[:, None, :],
                g,
                dense_full,
            ),
            2 * all_tokens * (width * (head_columns + HEAD) + 7 * length * HEAD),
            all_tokens * length,
        )

        live = dict(
            mixed=mixed, joined_grad=joined_grad, normed=normed, expanded=expanded, g=g, down=down_piece
        )

        def step(*landing, hold=()):
            fresh, held, views, outs, kept = fence(
                (
                    dict(live),
                    [chain.flight for chain in landing],
                    [chain.view for chain in waiting],
                    [chain.out for chain in chains],
                    [chain.held for chain in hold],
                )
            )
            for chain, one in zip(hold, kept):
                chain.held = one
            for chain, out in zip(chains, outs):
                chain.out = out
            live.update(fresh)
            for chain, one in zip(landing, held):
                chain.land(one)
            for chain, view in zip(waiting, views):
                chain.view = view
            waiting.clear()

        waiting, chains = [], []
        share_rows = cores * row_share

        def terms(*pairs):
            rows_tile = max(512, share_rows)
            group = rows_tile // share_rows
            groups = chips // group
            columns = sum(right.shape[1] for _, right in pairs)
            ins, args = [], []
            for left, right in pairs:
                ins += [pl.BlockSpec((all_tokens, rows_tile), lambda i: (0, i)), whole(right.shape)]
                args += [left, right]
            (view,) = run(
                terms_body,
                branches * groups,
                ins,
                [
                    (
                        pl.BlockSpec(
                            (group, 1, share_rows, columns), lambda i: (i % groups, i // groups, 0, 0)
                        ),
                        (chips, branches, share_rows, columns),
                        BF16,
                    )
                ],
                args,
                2 * all_tokens * width * columns,
            )
            chain = Chain(view, z, chips)
            waiting.append(chain)
            chains.append(chain)
            return chain

        def spread(chain):
            share = chain.total().reshape(branches * cores * row_share, -1)
            pieces = lax.all_to_all(share, ("branch", "core"), 0, 0, tiled=True)
            return pieces.reshape(branches * cores, row_share, -1)

        unit_flops = 2 * all_tokens * width * units
        big_tile = min(512, length)

        def hidden_values():
            return run(
                hidden_body,
                all_tokens // big_tile,
                [tile(big_tile, width), whole((width, units)), whole((1, units))],
                [(tile(big_tile, units), (all_tokens, units), BF16)] * 2,
                (live["expanded"], up_line, flat(up_bias_here)),
                unit_flops,
                2 * all_tokens * units,
            )

        def hidden_gradient():
            return run(
                hidden_grad_body,
                all_tokens // big_tile,
                [tile(big_tile, width), whole((units, width)), tile(big_tile, units)],
                [
                    (tile(big_tile, units), (all_tokens, units), BF16),
                    (whole((1, units)), (1, units), F32),
                ],
                (live["g"], down_line, live.pop("slope")),
                unit_flops,
            )

        blocks = branches * models

        def of_core(core, columns):
            return pl.BlockSpec((small_tile, columns), lambda i: (core * half_steps + i, 0))

        def out_blocks(pieces):
            steps = half_steps // pieces
            return (
                pl.BlockSpec((1, blocks, small_tile, span), lambda i: (i // steps, 0, i % steps, 0)),
                (pieces, blocks, tokens // pieces, span),
                BF16,
            )

        def input_terms(core, *got):
            return run(
                input_body,
                half_steps,
                [
                    tile(small_tile, width),
                    of_core(core, LANES),
                    of_core(core, head_columns),
                    whole((width, head_columns)),
                    of_core(core, units),
                    whole((width, units)),
                    whole((1, width)),
                    whole((1, width)),
                    *[out_blocks(2)[0]] * len(got),
                ],
                [out_blocks(2), (whole((4, width)), (4, width), F32)],
                (
                    (x_own, x_other)[core],
                    stats,
                    live["joined_grad"],
                    joined_full,
                    live["grad"],
                    up_line,
                    *gains,
                    *got,
                ),
                unit_flops // 2 + all_tokens * width * head_columns,
            )

        def forward_terms(core, *got):
            return run(
                forward_body,
                half_steps,
                [
                    of_core(core, HEAD),
                    whole((HEAD, width)),
                    of_core(core, units),
                    whole((units, width)),
                    *[out_blocks(1)[0]] * len(got),
                ],
                [out_blocks(1)],
                (live["mixed"], dense_full, live["active"], down_line, *got),
                unit_flops // 2 + all_tokens * width * HEAD,
            )[0]

        def block_sum(blocks):
            return lax.psum_scatter(blocks[0], ("branch", "mp"), scatter_dimension=0, tiled=True)[0]

        def first_sends(term):
            one, two = (term[h].reshape(branches, models, tokens // 2, span) for h in range(2))
            return partner(pick(one, 1 - b, 0), branch=1), partner(pick(two, 1 - m, 1), mp=1)

        def first_sum(term, got):
            one, two = (term[h].reshape(branches, models, tokens // 2, span) for h in range(2))
            return add_low(pick(one, b, 0), got[0]), add_low(pick(two, m, 1), got[1])

        def second_sends(pair):
            one, two = pair
            return partner(pick(one, 1 - m, 0), mp=1), partner(pick(two, 1 - b, 0), branch=1)

        def second_sum(pair, got):
            one, two = pair
            return jnp.concatenate(
                [
                    pick(one, m, 0).astype(F32) + got[0].astype(F32),
                    pick(two, b, 0).astype(F32) + got[1].astype(F32),
                ]
            )

        def put(pieces, shapes, layouts):
            return run(
                functools.partial(place_body, layouts),
                1,
                [whole(pieces.shape)],
                [(whole(shape), shape, F32) for shape in shapes],
                [pieces],
                0,
            )

        def unit_layouts(turned):
            return [
                (
                    k * part,
                    part,
                    0,
                    lambda device, k=k: (k * cores + device % cores) * branches + device // cores,
                    turned,
                )
                for k in range(chips)
            ]

        simple = part % LANES != 0 or row_share % 8 != 0

        def place_joined(pieces):
            if simple:
                pieces = pieces.astype(F32)
                joined = pieces[:, :, :head_columns].transpose(1, 0, 2).reshape(row_share, -1)
                return joined, pieces[:, :, head_columns:].transpose(0, 2, 1).reshape(-1, row_share)
            return put(
                pieces,
                [(row_share, heads * head_columns), (heads * HEAD, row_share)],
                [
                    (0, head_columns, 0, lambda device: device, False),
                    (head_columns, HEAD, 1, lambda device: device, True),
                ],
            )

        def place_units(pieces, turned):
            if not simple:
                shape = (hidden_columns, row_share) if turned else (row_share, hidden_columns)
                return put(pieces, [shape], unit_layouts(turned))[0]
            pieces = pieces.astype(F32).reshape(branches, cores, row_share, chips, part)
            if turned:
                return pieces.transpose(3, 1, 0, 4, 2).reshape(hidden_columns, row_share)
            return pieces.transpose(2, 3, 1, 0, 4).reshape(row_share, hidden_columns)

        def finish(chain):
            while chain.step < chips - 1:
                chain.send()
                step(chain)
            return spread(chain)

        step(up_line)
        up_line.send()
        joined_chain = terms((live.pop("normed"), live["joined_grad"]), (live["g"], live["mixed"]))
        joined_chain.send()
        step(up_line)
        down_line = Line(live.pop("down"), z, chips)
        down_line.send()
        live["active"], live["slope"] = hidden_values()
        down_chain = terms((live["g"], live["active"]))
        down_chain.prepare()
        step(down_line, joined_chain)
        down_line.send()
        down_chain.send()
        joined_chain.prepare()
        g_float = g_piece.astype(F32)
        out_slot = lax.dynamic_update_slice(
            jnp.zeros((width,), F32), jnp.sum(g_float, axis=0), (column_start,)
        )
        joined_slot = lax.dynamic_update_slice(
            jnp.zeros_like(joined_bias),
            joined_bias_grad.reshape(-1),
            ((m * heads + head_slot) * head_columns,),
        )
        live["slots"] = jnp.concatenate([out_slot, joined_slot])
        step(down_line, down_chain)
        down_line.send()
        joined_chain.send()
        down_chain.prepare()
        step(down_line, joined_chain)
        joined_chain.send()
        live["out_other"] = forward_terms(1)
        live["grad"], live["bias"] = hidden_gradient()
        step(joined_chain)
        down_chain.send()
        live["out_got"] = swap_core(live.pop("out_other"))
        live["joined_pieces"] = finish(joined_chain)
        up_chain = terms((live.pop("expanded"), live["grad"]))
        live.pop("g")
        up_chain.prepare()
        live["out"] = forward_terms(0, live.pop("out_got"))
        step(down_chain)
        forward_sum = block_sum(live.pop("out"))
        up_chain.send()
        down_chain.prepare()
        live["in_other"], live["sums_other"] = input_terms(1)
        step(up_chain)
        live["forward_sum"] = forward_sum
        down_chain.send()
        live["in_got"] = swap_core(live.pop("in_other"))
        up_chain.prepare()
        live["in"], live["sums_own"] = input_terms(0, live.pop("in_got"))
        up_slot = lax.dynamic_update_slice(
            jnp.zeros((models, chips, cores, branches, part), F32),
            live.pop("bias").reshape(1, chips, 1, 1, part),
            (m, 0, c, b, 0),
        ).reshape(-1)
        live["slots"] = jnp.concatenate([live["slots"], up_slot])
        step(down_chain)
        up_chain.send()
        live["in_got"] = first_sends(live["in"])
        sums = live.pop("sums_own") + live.pop("sums_other")
        small = jnp.concatenate([sums.reshape(-1), live.pop("slots")])
        small = (
            small
            + partner(small, core=1)
            + partner(small, branch=1)
            + partner(small, branch=1, core=1)
        )
        live["joined_out"], live["dense_out"] = place_joined(live.pop("joined_pieces"))
        down_pieces = finish(down_chain)
        step(up_chain)
        up_chain.prepare()
        step()
        live["down_pieces"] = down_pieces
        up_chain.send()
        live["in"] = first_sum(live["in"], live.pop("in_got"))
        live["in_got"] = second_sends(live["in"])
        near = lax.ppermute(small, "z", [(i, i ^ 1) for i in range(chips)])
        far = [
            lax.ppermute(
                small,
                ("mp", "z"),
                [
                    (one * chips + i, (1 - one) * chips + (i ^ flip))
                    for one in range(models)
                    for i in range(chips)
                ],
            )
            for flip in range(2)
        ]
        live["small"] = small + near + far[0] + far[1]
        forward_sum = live["forward_sum"]
        residual = columns_of(x_own, column_start, span).astype(F32)
        column_bias = columns_of(dense_bias + down_bias, column_start, span)
        block_output = (residual + forward_sum + column_bias).astype(BF16)
        live["block_output"] = block_output
        step(up_chain)
        block_output = live["block_output"]
        up_pieces = finish(up_chain)
        small = live["small"]
        flip = 2
        while flip < chips:
            small = small + lax.ppermute(small, "z", [(i, i ^ flip) for i in range(chips)])
            flip *= 2
        input_sum = second_sum(live.pop("in"), live.pop("in_got"))
        joined_out, dense_out = live["joined_out"], live["dense_out"]
        down_out, up_out = place_units(live["down_pieces"], True), place_units(up_pieces, False)

        input_gradient = (g_float + input_sum).astype(BF16)

        w = width
        joined_end = 5 * w + joined_bias.shape[0]
        return (
            block_output.reshape(rows, length, span),
            input_gradient.reshape(rows, length, span),
            small[:w],
            small[w : 2 * w],
            joined_out,
            small[5 * w : joined_end],
            dense_out,
            small[4 * w : 5 * w],
            small[2 * w : 3 * w],
            small[3 * w : 4 * w],
            up_out,
            small[joined_end:],
            down_out,
            small[4 * w : 5 * w],
        )

    data = ("z", "core")
    everything = ("branch", "z", "core")
    in_specs = (
        P(data, None, None),
        P(data, None, ("branch", "mp")),
        P(data, None),
        P(),
        P(),
        P(data, "mp"),
        P(),
        P(("mp", "z", "core"), None),
        P(),
        P(),
        P(),
        P(data, "mp"),
        P(),
        P(("mp", "z", "core"), None),
        P(),
    )
    out_specs = (
        P(data, None, ("branch", "mp")),
        P(data, None, ("branch", "mp")),
        P(),
        P(),
        P(everything, "mp"),
        P(),
        P("mp", everything),
        P(),
        P(),
        P(),
        P(everything, "mp"),
        P(),
        P("mp", everything),
        P(),
    )
    return jax.shard_map(
        on_device, mesh=fine, in_specs=in_specs, out_specs=out_specs, check_vma=False
    )
```

profile of v0, /device:TPU:0, one launch (start us, length us, event | category | flops | bytes accessed | tf_op | source)
XLA Modules:
  0.0 541.2 jit_solution(13756812006737311752)
XLA Ops:
  9.1 6.0 %collective-permute-done.1 = bf16[256,768]{1,0:T(8,128)(2,1)S(1)} collective-permute-done((bf16[256,768]{1,0:T(8,128)(2,1)S(1)}, bf16[256,768]{1,0:T(8,128)(2,1)S(1)}, u32[]{:S(2)}, u32[]{:S(2)}) %collective-permute-start.1) | collective-permute-done | bytes 393248 | tf_op jit(solution)/shard_map/ppermute | solution.py:427
  28.1 5.4 multiply_sine_fusion
  33.4 5.3 collective-permute-done.3
  41.2 12.2 %collective-permute-start.8 = (bf16[256,1024]{1,0:T(8,128)(2,1)S(1)}, bf16[256,1024]{1,0:T(8,128)(2,1)S(1)}, u32[]{:S(2)}, u32[]{:S(2)}) collective-permute-start(bf16[256,1024]{1,0:T(8,128)(2,1)S(1)} %pad_maximum_fusion.1), channel_id=1, source_target_pairs={{0,1},{1,0},{2,3},{3,2},{4,5},{5,4},{6,7},{7,6},{8,9},{9,8},{10,11... | collective-permute-start | bytes 1572872 | tf_op jit(solution)/shard_map/ppermute | solution.py:427
  56.0 14.5 %shard_map.254 = (bf16[2048,2048]{1,0:T(8,128)(2,1)}, bf16[2048,2048]{1,0:T(8,128)(2,1)}, f32[2048,128]{1,0:T(8,128)}) custom-call(bf16[1024,2048]{1,0:T(8,128)(2,1)} %bitcast.113, bf16[1024,2048]{1,0:T(8,128)(2,1)} %collective-permute-done.other_ref.refs_0_, f32[1,2048]{1,0:T(1,128)} %bitcast.127, f32[1,2048]{1,0:T(1,128)} %bitcast.135, ...), custom_call_target="tpu_custom_call" | custom-call | flops 1310720 | bytes 410112 | tf_op jit(solution)/shard_map/pallas_call | solution.py:69
  74.1 18.3 %collective-permute-start.9 = (bf16[512,1024]{1,0:T(8,128)(2,1)S(1)}, bf16[512,1024]{1,0:T(8,128)(2,1)}, u32[]{:S(2)}, u32[]{:S(2)}) collective-permute-start(bf16[512,1024]{1,0:T(8,128)(2,1)S(1)} %maximum_select_fusion.refs_4_.refs_8_), channel_id=1, source_target_pairs={{0,2},{2,4},{4,6},{1,3},{3,5},{5,7},{8,10},{10,12},{12,14},{9,11},... | collective-permute-start | bytes 3145736 | tf_op jit(solution)/shard_map/ppermute | solution.py:366
  92.9 9.6 %shard_map.255.g_ref.refs_2_.refs_0_ = bf16[2048,2048]{1,0:T(8,128)(2,1)} custom-call(s32[4]{0:T(128)} %pad_add_fusion.1.starts_ref, bf16[1024,512]{1,0:T(8,128)(2,1)} %bitcast.6.refs_0_, bf16[1024,512]{1,0:T(8,128)(2,1)} %collective-permute-done.11.refs_1_, bf16[1024,512]{1,0:T(8,128)(2,1)} %collective-permute-done.5.refs_2_, ...), custom_call_target="tpu_custom_call" | custom-call | flops 65536 | bytes 262144 | tf_op jit(solution)/shard_map/pallas_call | solution.py:69
  102.6 28.8 %all-gather.5.cloned.1.call-done.dense_ref.refs_1_ = bf16[256,2048]{1,0:T(8,128)(2,1)} async-done(((bf16[64,2048]{1,0:T(8,128)(2,1)}), bf16[256,2048]{1,0:T(8,128)(2,1)}) %all-gather.5.cloned.1.call-update) | async-done | bytes 1048592 | tf_op jit(solution)/shard_map/all_gather | solution.py:448
  136.7 24.1 %shard_map.256 = (bf16[2048,256]{1,0:T(8,128)(2,1)}, bf16[2048,768]{1,0:T(8,128)(2,1)}, f32[1,768]{1,0:T(1,128)}) custom-call(bf16[2048,2048]{1,0:T(8,128)(2,1)} %get-tuple-element.211.normed_ref.refs_0_, bf16[2048,768]{1,0:T(8,128)(2,1)} %all-gather.3.cloned.1.call-done.joined_ref.refs_3_, f32[1,768]{1,0:T(1,128)} %reshape.166.bias_ref, ...), custom_call_target="tpu_custom_call" | custom-call | flops 192937984 | bytes 442720 | tf_op jit(solution)/shard_map/pallas_call | solution.py:69
  164.4 14.4 %shard_map.257 = bf16[4,2,256,1024]{3,2,1,0:T(8,128)(2,1)} custom-call(bf16[2048,2048]{1,0:T(8,128)(2,1)} %get-tuple-element.211.normed_ref.refs_0_, bf16[2048,768]{1,0:T(8,128)(2,1)} %get-tuple-element.290.refs_1_.refs_2_, bf16[2048,2048]{1,0:T(8,128)(2,1)} %shard_map.255.g_ref.refs_2_.refs_0_, bf16[2048,256]{1,0:T(8,128)(2,1)} %get-tuple-element.270.refs_3_.refs_0_), custom_call_target="tpu_custom_call" | custom-call | flops 134217728 | bytes 393216 | tf_op jit(solution)/shard_map/pallas_call | solution.py:69
  183.4 9.1 %collective-permute-start.21 = (bf16[2,256,1024]{2,1,0:T(8,128)(2,1)}, bf16[2,256,1024]{2,1,0:T(8,128)(2,1)}, u32[]{:S(2)}, u32[]{:S(2)}) collective-permute-start(bf16[2,256,1024]{2,1,0:T(8,128)(2,1)} %get-tuple-element.363), channel_id=1, source_target_pairs={{0,2},{1,3},{8,10},{9,11},{16,18},{17,19},{24,26},{25,27}} | collective-permute-start | bytes 3145736 | tf_op jit(solution)/shard_map/ppermute | solution.py:339
  194.8 4.6 collective-permute-start.19
  200.9 17.5 %shard_map.258 = (bf16[2048,1024]{1,0:T(8,128)(2,1)}, bf16[2048,1024]{1,0:T(8,128)(2,1)}) custom-call(s32[1]{0:T(128)} %bitcast.1.index_ref, bf16[2048,2048]{1,0:T(8,128)(2,1)} %get-tuple-element.275.refs_0_, bf16[512,1024]{1,0:T(8,128)(2,1)} %copy-done.14, bf16[512,1024]{1,0:T(8,128)(2,1)} %copy-done.13, ...), custom_call_target="tpu_custom_call" | custom-call | flops 134217728 | bytes 376896 | tf_op jit(solution)/shard_map/pallas_call | solution.py:69
  218.4 13.4 %shard_map.259 = bf16[4,2,256,1024]{3,2,1,0:T(8,128)(2,1)} custom-call(bf16[2048,2048]{1,0:T(8,128)(2,1)} %shard_map.255.g_ref.refs_2_.refs_0_, bf16[2048,1024]{1,0:T(8,128)(2,1)} %get-tuple-element.264.refs_1_.refs_2_), custom_call_target="tpu_custom_call" | custom-call | flops 134217728 | bytes 262144 | tf_op jit(solution)/shard_map/pallas_call | solution.py:69
  235.6 5.4 collective-permute-start.25
  251.2 9.7 %collective-permute-done.25 = bf16[2,256,1024]{2,1,0:T(8,128)(2,1)} collective-permute-done((bf16[2,256,1024]{2,1,0:T(8,128)(2,1)}, bf16[2,256,1024]{2,1,0:T(8,128)(2,1)}, u32[]{:S(2)}, u32[]{:S(2)}) %collective-permute-start.25) | collective-permute-done | bytes 1048608 | tf_op jit(solution)/shard_map/ppermute | solution.py:339
  260.9 7.2 %collective-permute-done.24.refs_6_.refs_8_ = bf16[256,2048]{1,0:T(8,128)(2,1)} collective-permute-done((bf16[256,2048]{1,0:T(8,128)(2,1)S(1)}, bf16[256,2048]{1,0:T(8,128)(2,1)}, u32[]{:S(2)}, u32[]{:S(2)}) %collective-permute-start.24) | collective-permute-done | bytes 1048608 | tf_op jit(solution)/shard_map/ppermute | solution.py:367
  276.0 4.7 fusion.17
  280.7 10.0 %collective-permute-done.29 = bf16[2,256,1024]{2,1,0:T(8,128)(2,1)} collective-permute-done((bf16[2,256,1024]{2,1,0:T(8,128)(2,1)}, bf16[2,256,1024]{2,1,0:T(8,128)(2,1)}, u32[]{:S(2)}, u32[]{:S(2)}) %collective-permute-start.29) | collective-permute-done | bytes 1048608 | tf_op jit(solution)/shard_map/ppermute | solution.py:339
  290.7 7.4 %collective-permute-done.28.refs_7_.refs_9_ = bf16[256,2048]{1,0:T(8,128)(2,1)S(1)} collective-permute-done((bf16[256,2048]{1,0:T(8,128)(2,1)}, bf16[256,2048]{1,0:T(8,128)(2,1)S(1)}, u32[]{:S(2)}, u32[]{:S(2)}) %collective-permute-start.28) | collective-permute-done | bytes 1048608 | tf_op jit(solution)/shard_map/ppermute | solution.py:367
  302.3 4.8 collective-permute-start.31
  307.2 11.0 %shard_map.261 = bf16[1,4,1024,512]{3,2,1,0:T(8,128)(2,1)} custom-call(s32[1]{0:T(128)} %bitcast.1.index_ref, bf16[2048,256]{1,0:T(8,128)(2,1)} %get-tuple-element.270.refs_3_.refs_0_, bf16[256,2048]{1,0:T(8,128)(2,1)} %all-gather.5.cloned.1.call-done.dense_ref.refs_1_, bf16[2048,1024]{1,0:T(8,128)(2,1)} %get-tuple-element.264.refs_1_.refs_2_, ...), custom_call_target="tpu_custom_call" | custom-call | flops 83886080 | bytes 278528 | tf_op jit(solution)/shard_map/pallas_call | solution.py:69
  318.2 15.2 %shard_map.260 = (bf16[2048,1024]{1,0:T(8,128)(2,1)}, f32[1,1024]{1,0:T(1,128)}) custom-call(s32[1]{0:T(128)} %bitcast.1.index_ref, bf16[2048,2048]{1,0:T(8,128)(2,1)} %shard_map.255.g_ref.refs_2_.refs_0_, bf16[256,2048]{1,0:T(8,128)(2,1)} %copy-done.10, bf16[256,2048]{1,0:T(8,128)(2,1)} %copy-done.9, bf16[256,2048]{1,0:T(8,128)(2,1)} %copy-done.8, ...), custom_call_target="tpu_custom_call" | custom-call | flops 134217728 | bytes 376896 | tf_op jit(solution)/shard_map/pallas_call | solution.py:69
  344.7 13.4 %shard_map.263 = bf16[4,2,256,1024]{3,2,1,0:T(8,128)(2,1)} custom-call(bf16[2048,2048]{1,0:T(8,128)(2,1)} %get-tuple-element.275.refs_0_, bf16[2048,1024]{1,0:T(8,128)(2,1)} %get-tuple-element.289.refs_1_.refs_4_), custom_call_target="tpu_custom_call" | custom-call | flops 134217728 | bytes 262144 | tf_op jit(solution)/shard_map/pallas_call | solution.py:69
  359.9 11.6 %shard_map.262 = bf16[1,4,1024,512]{3,2,1,0:T(8,128)(2,1)} custom-call(s32[1]{0:T(128)} %bitcast.1.index_ref, bf16[2048,256]{1,0:T(8,128)(2,1)} %get-tuple-element.270.refs_3_.refs_0_, bf16[256,2048]{1,0:T(8,128)(2,1)} %all-gather.5.cloned.1.call-done.dense_ref.refs_1_, bf16[2048,1024]{1,0:T(8,128)(2,1)} %get-tuple-element.264.refs_1_.refs_2_, ...), custom_call_target="tpu_custom_call" | custom-call | flops 83886080 | bytes 344064 | tf_op jit(solution)/shard_map/pallas_call | solution.py:69
  375.6 18.6 %shard_map.264 = (bf16[2,4,512,512]{3,2,1,0:T(8,128)(2,1)}, f32[4,2048]{1,0:T(4,128)}) custom-call(s32[1]{0:T(128)} %bitcast.1.index_ref, bf16[1024,2048]{1,0:T(8,128)(2,1)} %collective-permute-done.other_ref.refs_0_, f32[2048,128]{1,0:T(8,128)} %get-tuple-element.279.refs_1_, bf16[2048,768]{1,0:T(8,128)(2,1)} %get-tuple-element.290.refs_1_.refs_2_, ...), custom_call_target="tpu_custom_call" | custom-call | flops 117440512 | bytes 426752 | tf_op jit(solution)/shard_map/pallas_call | solution.py:69
  408.9 18.8 %shard_map.265 = (bf16[2,4,512,512]{3,2,1,0:T(8,128)(2,1)}, f32[4,2048]{1,0:T(4,128)}) custom-call(s32[1]{0:T(128)} %bitcast.1.index_ref, bf16[1024,2048]{1,0:T(8,128)(2,1)} %bitcast.114, f32[2048,128]{1,0:T(8,128)} %get-tuple-element.279.refs_1_, bf16[2048,768]{1,0:T(8,128)(2,1)} %get-tuple-element.290.refs_1_.refs_2_, ...), custom_call_target="tpu_custom_call" | custom-call | flops 117440512 | bytes 492288 | tf_op jit(solution)/shard_map/pallas_call | solution.py:69
  433.5 4.8 collective-permute-start.43
  461.4 4.8 collective-permute-start.50
  473.1 5.0 fusion.7
  490.5 9.1 %collective-permute-done.46 = bf16[512,512]{1,0:T(8,128)(2,1)S(1)} collective-permute-done((bf16[512,512]{1,0:T(8,128)(2,1)S(1)}, bf16[512,512]{1,0:T(8,128)(2,1)S(1)}, u32[]{:S(2)}, u32[]{:S(2)}) %collective-permute-start.46) | collective-permute-done | bytes 524320 | tf_op jit(solution)/shard_map/ppermute | solution.py:427
  503.3 5.1 collective-permute-done.54
  (259 shorter events, 176.4 us)
Async XLA Ops:
  7.2 95.4 %all-gather.3.cloned.1.call-start = ((), (), s32[]{:S(2)}) async-start(), calls=%async_computation.4 | async-start | bytes 3932160 | tf_op jit(solution)/shard_map/all_gather | solution.py:448
  7.3 32.4 %collective-permute-start = (bf16[1024,2048]{1,0:T(8,128)(2,1)}, bf16[1024,2048]{1,0:T(8,128)(2,1)}, u32[]{:S(2)}, u32[]{:S(2)}) collective-permute-start(bf16[1024,2048]{1,0:T(8,128)(2,1)} %bitcast.112), channel_id=1, source_target_pairs={{0,1},{1,0},{2,3},{3,2},{4,5},{5,4},{6,7},{7,6},{8,9},{9,8},{10,11... | collective-permute-start | bytes 12582920 | tf_op jit(solution)/shard_map/ppermute | solution.py:427
  16.3 115.0 %all-gather.5.cloned.1.call-start = ((), (), s32[]{:S(2)}) async-start(), calls=%async_computation.5 | async-start | bytes 1310720 | tf_op jit(solution)/shard_map/all_gather | solution.py:448
  16.4 54.6 %collective-permute-start.7 = (bf16[1024,512]{1,0:T(8,128)(2,1)}, bf16[1024,512]{1,0:T(8,128)(2,1)}, u32[]{:S(2)}, u32[]{:S(2)}) collective-permute-start(bf16[1024,512]{1,0:T(8,128)(2,1)} %bitcast.6.refs_0_), channel_id=1, source_target_pairs={{0,24},{8,16},{16,8},{24,0},{1,25},{9,17},{17,9},{25,1},{2,26},{10... | collective-permute-start | bytes 3145736 | tf_op jit(solution)/shard_map/ppermute | solution.py:427
  20.3 50.7 %collective-permute-start.6 = (bf16[1024,512]{1,0:T(8,128)(2,1)}, bf16[1024,512]{1,0:T(8,128)(2,1)}, u32[]{:S(2)}, u32[]{:S(2)}) collective-permute-start(bf16[1024,512]{1,0:T(8,128)(2,1)} %bitcast.6.refs_0_), channel_id=1, source_target_pairs={{0,16},{16,0},{1,17},{17,1},{2,18},{18,2},{3,19},{19,3},{4,20},{20... | collective-permute-start | bytes 3145736 | tf_op jit(solution)/shard_map/ppermute | solution.py:427
  38.8 32.2 %collective-permute-start.5 = (bf16[1024,512]{1,0:T(8,128)(2,1)}, bf16[1024,512]{1,0:T(8,128)(2,1)}, u32[]{:S(2)}, u32[]{:S(2)}) collective-permute-start(bf16[1024,512]{1,0:T(8,128)(2,1)} %bitcast.6.refs_0_), channel_id=1, source_target_pairs={{0,8},{8,0},{1,9},{9,1},{2,10},{10,2},{3,11},{11,3},{4,12},{12,4},... | collective-permute-start | bytes 3145736 | tf_op jit(solution)/shard_map/ppermute | solution.py:427
  41.2 29.3 %collective-permute-start.8 = (bf16[256,1024]{1,0:T(8,128)(2,1)S(1)}, bf16[256,1024]{1,0:T(8,128)(2,1)S(1)}, u32[]{:S(2)}, u32[]{:S(2)}) collective-permute-start(bf16[256,1024]{1,0:T(8,128)(2,1)S(1)} %pad_maximum_fusion.1), channel_id=1, source_target_pairs={{0,1},{1,0},{2,3},{3,2},{4,5},{5,4},{6,7},{7,6},{8,9},{9,8},{10,11... | collective-permute-start | bytes 1572872 | tf_op jit(solution)/shard_map/ppermute | solution.py:427
  72.2 59.2 %collective-permute-start.10 = (bf16[512,1024]{1,0:T(8,128)(2,1)S(1)}, bf16[512,1024]{1,0:T(8,128)(2,1)S(1)}, u32[]{:S(2)}, u32[]{:S(2)}) collective-permute-start(bf16[512,1024]{1,0:T(8,128)(2,1)S(1)} %maximum_select_fusion.refs_4_.refs_8_), channel_id=1, source_target_pairs={{2,0},{4,2},{6,4},{3,1},{5,3},{7,5},{10,8},{12,10},{14,12},{11,9},... | collective-permute-start | bytes 3145736 | tf_op jit(solution)/shard_map/ppermute | solution.py:367
  74.1 57.3 %collective-permute-start.9 = (bf16[512,1024]{1,0:T(8,128)(2,1)S(1)}, bf16[512,1024]{1,0:T(8,128)(2,1)}, u32[]{:S(2)}, u32[]{:S(2)}) collective-permute-start(bf16[512,1024]{1,0:T(8,128)(2,1)S(1)} %maximum_select_fusion.refs_4_.refs_8_), channel_id=1, source_target_pairs={{0,2},{2,4},{4,6},{1,3},{3,5},{5,7},{8,10},{10,12},{12,14},{9,11},... | collective-permute-start | bytes 3145736 | tf_op jit(solution)/shard_map/ppermute | solution.py:366
  131.4 29.5 %collective-permute-start.15 = (bf16[512,1024]{1,0:T(8,128)(2,1)}, bf16[512,1024]{1,0:T(8,128)(2,1)S(1)}, u32[]{:S(2)}, u32[]{:S(2)}) collective-permute-start(bf16[512,1024]{1,0:T(8,128)(2,1)} %collective-permute-done.9.refs_3_.refs_7_), channel_id=1, source_target_pairs={{2,4},{4,6},{3,5},{5,7},{10,12},{12,14},{11,13},{13,15},{18,20},{2... | collective-permute-start | bytes 3145736 | tf_op jit(solution)/shard_map/ppermute | solution.py:366
  132.1 30.1 %collective-permute-start.16 = (bf16[512,1024]{1,0:T(8,128)(2,1)S(1)}, bf16[512,1024]{1,0:T(8,128)(2,1)}, u32[]{:S(2)}, u32[]{:S(2)}) collective-permute-start(bf16[512,1024]{1,0:T(8,128)(2,1)S(1)} %collective-permute-done.10.refs_5_.refs_9_), channel_id=1, source_target_pairs={{2,0},{4,2},{3,1},{5,3},{10,8},{12,10},{11,9},{13,11},{18,16},{20,... | collective-permute-start | bytes 3145736 | tf_op jit(solution)/shard_map/ppermute | solution.py:367
  162.2 30.3 %collective-permute-start.17 = (bf16[512,1024]{1,0:T(8,128)(2,1)S(1)}, bf16[512,1024]{1,0:T(8,128)(2,1)S(1)}, u32[]{:S(2)}, u32[]{:S(2)}) collective-permute-start(bf16[512,1024]{1,0:T(8,128)(2,1)S(1)} %collective-permute-done.15.refs_2_.refs_6_), channel_id=1, source_target_pairs={{4,6},{5,7},{12,14},{13,15},{20,22},{21,23},{28,30},{29,31}} | collective-permute-start | bytes 3145736 | tf_op jit(solution)/shard_map/ppermute | solution.py:366
  162.9 29.6 %collective-permute-start.18 = (bf16[512,1024]{1,0:T(8,128)(2,1)}, bf16[512,1024]{1,0:T(8,128)(2,1)}, u32[]{:S(2)}, u32[]{:S(2)}) collective-permute-start(bf16[512,1024]{1,0:T(8,128)(2,1)} %collective-permute-done.16.refs_6_.refs_10_), channel_id=1, source_target_pairs={{2,0},{3,1},{10,8},{11,9},{18,16},{19,17},{26,24},{27,25}} | collective-permute-start | bytes 3145736 | tf_op jit(solution)/shard_map/ppermute | solution.py:367
  181.8 53.2 %collective-permute-start.22 = (bf16[2,256,1024]{2,1,0:T(8,128)(2,1)}, bf16[2,256,1024]{2,1,0:T(8,128)(2,1)}, u32[]{:S(2)}, u32[]{:S(2)}) collective-permute-start(bf16[2,256,1024]{2,1,0:T(8,128)(2,1)} %get-tuple-element.362), channel_id=1, source_target_pairs={{6,4},{7,5},{14,12},{15,13},{22,20},{23,21},{30,28},{31,29}} | collective-permute-start | bytes 3145736 | tf_op jit(solution)/shard_map/ppermute | solution.py:340
  183.4 51.6 %collective-permute-start.21 = (bf16[2,256,1024]{2,1,0:T(8,128)(2,1)}, bf16[2,256,1024]{2,1,0:T(8,128)(2,1)}, u32[]{:S(2)}, u32[]{:S(2)}) collective-permute-start(bf16[2,256,1024]{2,1,0:T(8,128)(2,1)} %get-tuple-element.363), channel_id=1, source_target_pairs={{0,2},{1,3},{8,10},{9,11},{16,18},{17,19},{24,26},{25,27}} | collective-permute-start | bytes 3145736 | tf_op jit(solution)/shard_map/ppermute | solution.py:339
  193.5 41.5 %collective-permute-start.20 = (bf16[256,2048]{1,0:T(8,128)(2,1)S(1)}, bf16[256,2048]{1,0:T(8,128)(2,1)S(1)}, u32[]{:S(2)}, u32[]{:S(2)}) collective-permute-start(bf16[256,2048]{1,0:T(8,128)(2,1)S(1)} %constant_dynamic-slice_fusion.refs_4_.refs_6_), channel_id=1, source_target_pairs={{2,0},{4,2},{6,4},{3,1},{5,3},{7,5},{10,8},{12,10},{14,12},{11,9},... | collective-permute-start | bytes 3145736 | tf_op jit(solution)/shard_map/ppermute | solution.py:367
  194.8 40.8 %collective-permute-start.19 = (bf16[256,2048]{1,0:T(8,128)(2,1)S(1)}, bf16[256,2048]{1,0:T(8,128)(2,1)S(1)}, u32[]{:S(2)}, u32[]{:S(2)}) collective-permute-start(bf16[256,2048]{1,0:T(8,128)(2,1)S(1)} %constant_dynamic-slice_fusion.refs_4_.refs_6_), channel_id=1, source_target_pairs={{0,2},{2,4},{4,6},{1,3},{3,5},{5,7},{8,10},{10,12},{12,14},{9,11},... | collective-permute-start | bytes 3145736 | tf_op jit(solution)/shard_map/ppermute | solution.py:366
  301.0 32.4 %collective-permute-start.32 = (bf16[2,256,1024]{2,1,0:T(8,128)(2,1)S(1)}, bf16[2,256,1024]{2,1,0:T(8,128)(2,1)S(1)}, u32[]{:S(2)}, u32[]{:S(2)}) collective-permute-start(bf16[2,256,1024]{2,1,0:T(8,128)(2,1)S(1)} %get-tuple-element.354), channel_id=1, source_target_pairs={{6,4},{4,2},{2,0},{7,5},{5,3},{3,1},{14,12},{12,10},{10,8},{15,13}... | collective-permute-start | bytes 3145736 | tf_op jit(solution)/shard_map/ppermute | solution.py:340
  302.3 31.1 %collective-permute-start.31 = (bf16[2,256,1024]{2,1,0:T(8,128)(2,1)S(1)}, bf16[2,256,1024]{2,1,0:T(8,128)(2,1)S(1)}, u32[]{:S(2)}, u32[]{:S(2)}) collective-permute-start(bf16[2,256,1024]{2,1,0:T(8,128)(2,1)S(1)} %get-tuple-element.355), channel_id=1, source_target_pairs={{0,2},{2,4},{4,6},{1,3},{3,5},{5,7},{8,10},{10,12},{12,14},{9,11},... | collective-permute-start | bytes 3145736 | tf_op jit(solution)/shard_map/ppermute | solution.py:339
  333.4 26.5 %collective-permute-start.33 = (bf16[1,4,1024,512]{3,2,1,0:T(8,128)(2,1)}, bf16[1,4,1024,512]{3,2,1,0:T(8,128)(2,1)}, u32[]{:S(2)}, u32[]{:S(2)}) collective-permute-start(bf16[1,4,1024,512]{3,2,1,0:T(8,128)(2,1)} %shard_map.261), channel_id=1, source_target_pairs={{0,1},{1,0},{2,3},{3,2},{4,5},{5,4},{6,7},{7,6},{8,9},{9,8},{10,11... | collective-permute-start | bytes 12582920 | tf_op jit(solution)/shard_map/ppermute | solution.py:427
  333.5 38.1 %collective-permute-start.34 = (bf16[2,256,1024]{2,1,0:T(8,128)(2,1)}, bf16[2,256,1024]{2,1,0:T(8,128)(2,1)}, u32[]{:S(2)}, u32[]{:S(2)}) collective-permute-start(bf16[2,256,1024]{2,1,0:T(8,128)(2,1)} %get-tuple-element.273), channel_id=1, source_target_pairs={{0,2},{2,4},{1,3},{3,5},{8,10},{10,12},{9,11},{11,13},{16,18},{18,... | collective-permute-start | bytes 3145736 | tf_op jit(solution)/shard_map/ppermute | solution.py:339
  336.3 35.2 %collective-permute-start.35 = (bf16[2,256,1024]{2,1,0:T(8,128)(2,1)}, bf16[2,256,1024]{2,1,0:T(8,128)(2,1)}, u32[]{:S(2)}, u32[]{:S(2)}) collective-permute-start(bf16[2,256,1024]{2,1,0:T(8,128)(2,1)} %get-tuple-element.274), channel_id=1, source_target_pairs={{6,4},{4,2},{7,5},{5,3},{14,12},{12,10},{15,13},{13,11},{22,20},{2... | collective-permute-start | bytes 3145736 | tf_op jit(solution)/shard_map/ppermute | solution.py:340
  340.9 30.7 %all-to-all-start = ((bf16[4,128,1024]{2,1,0:T(8,128)(2,1)}), bf16[4,128,1024]{2,1,0:T(8,128)(2,1)S(1)}, u32[]{:S(2)}, u32[]{:S(2)}) async-start(bf16[4,128,1024]{2,1,0:T(8,128)(2,1)} %bitcast.24), calls=%async_computation | async-start | bytes 2097152 | tf_op jit(solution)/shard_map/all_to_all | solution.py:630
  344.7 86.1 %reduce-scatter.4.cloned.1.call-start = ((), (), s32[]{:S(2)}) async-start(), calls=%async_computation.6 | async-start | bytes 5242880
  399.0 28.6 %collective-permute-start.39 = (bf16[2,256,1024]{2,1,0:T(8,128)(2,1)}, bf16[2,256,1024]{2,1,0:T(8,128)(2,1)S(1)}, u32[]{:S(2)}, u32[]{:S(2)}) collective-permute-start(bf16[2,256,1024]{2,1,0:T(8,128)(2,1)} %get-tuple-element.298), channel_id=1, source_target_pairs={{0,2},{2,4},{4,6},{1,3},{3,5},{5,7},{8,10},{10,12},{12,14},{9,11},... | collective-permute-start | bytes 3145736 | tf_op jit(solution)/shard_map/ppermute | solution.py:339
  402.7 28.1 %collective-permute-start.40 = (bf16[2,256,1024]{2,1,0:T(8,128)(2,1)}, bf16[2,256,1024]{2,1,0:T(8,128)(2,1)S(1)}, u32[]{:S(2)}, u32[]{:S(2)}) collective-permute-start(bf16[2,256,1024]{2,1,0:T(8,128)(2,1)} %get-tuple-element.299), channel_id=1, source_target_pairs={{6,4},{4,2},{2,0},{7,5},{5,3},{3,1},{14,12},{12,10},{10,8},{15,13}... | collective-permute-start | bytes 3145736 | tf_op jit(solution)/shard_map/ppermute | solution.py:340
  433.5 27.6 %collective-permute-start.43 = (bf16[2,256,1024]{2,1,0:T(8,128)(2,1)}, bf16[2,256,1024]{2,1,0:T(8,128)(2,1)}, u32[]{:S(2)}, u32[]{:S(2)}) collective-permute-start(bf16[2,256,1024]{2,1,0:T(8,128)(2,1)} %get-tuple-element.308), channel_id=1, source_target_pairs={{0,2},{2,4},{1,3},{3,5},{8,10},{10,12},{9,11},{11,13},{16,18},{18,... | collective-permute-start | bytes 3145736 | tf_op jit(solution)/shard_map/ppermute | solution.py:339
  444.8 28.3 %collective-permute-start.42 = (bf16[2,512,512]{2,1,0:T(8,128)(2,1)}, bf16[2,512,512]{2,1,0:T(8,128)(2,1)S(1)}, u32[]{:S(2)}, u32[]{:S(2)}) collective-permute-start(bf16[2,512,512]{2,1,0:T(8,128)(2,1)} %dynamic-slice_bitcast_fusion), channel_id=1, source_target_pairs={{0,8},{8,0},{1,9},{9,1},{2,10},{10,2},{3,11},{11,3},{4,12},{12,4},... | collective-permute-start | bytes 3145736 | tf_op jit(solution)/shard_map/ppermute | solution.py:427
  449.4 41.1 %all-to-all-start.1 = ((bf16[4,128,1024]{2,1,0:T(8,128)(2,1)}), bf16[4,128,1024]{2,1,0:T(8,128)(2,1)S(1)}, u32[]{:S(2)}, u32[]{:S(2)}) async-start(bf16[4,128,1024]{2,1,0:T(8,128)(2,1)} %bitcast.42), calls=%async_computation.1 | async-start | bytes 2097152 | tf_op jit(solution)/shard_map/all_to_all | solution.py:630
  455.6 30.6 %collective-permute-start.52 = (f32[24576]{0:T(1024)S(1)}, f32[24576]{0:T(1024)S(1)}, u32[]{:S(2)}, u32[]{:S(2)}) collective-permute-start(f32[24576]{0:T(1024)S(1)} %add_add_fusion.1), channel_id=1, source_target_pairs={{0,10},{2,8},{4,14},{6,12},{8,2},{10,0},{12,6},{14,4},{1,11},{3,9}... | collective-permute-start | bytes 294920 | tf_op jit(solution)/shard_map/ppermute | solution.py:874
  461.4 26.5 %collective-permute-start.50 = (f32[24576]{0:T(1024)S(1)}, f32[24576]{0:T(1024)S(1)}, u32[]{:S(2)}, u32[]{:S(2)}) collective-permute-start(f32[24576]{0:T(1024)S(1)} %add_add_fusion.1), channel_id=1, source_target_pairs={{0,2},{2,0},{4,6},{6,4},{1,3},{3,1},{5,7},{7,5},{8,10},{10,8},{12,... | collective-permute-start | bytes 294920 | tf_op jit(solution)/shard_map/ppermute | solution.py:872
  481.7 26.7 %collective-permute-start.54 = (bf16[2,256,1024]{2,1,0:T(8,128)(2,1)}, bf16[2,256,1024]{2,1,0:T(8,128)(2,1)}, u32[]{:S(2)}, u32[]{:S(2)}) collective-permute-start(bf16[2,256,1024]{2,1,0:T(8,128)(2,1)} %get-tuple-element.330), channel_id=1, source_target_pairs={{6,4},{4,2},{2,0},{7,5},{5,3},{3,1},{14,12},{12,10},{10,8},{15,13}... | collective-permute-start | bytes 3145736 | tf_op jit(solution)/shard_map/ppermute | solution.py:340
  (67 other events, 1078.3 us)
Sparse Core Ops, SparseCore 0:
  16.5 70.5 all-gather.2
  89.2 42.0 all-gather.4
  371.7 50.9 reduce-scatter.3
where the time goes:
time: 551 us; the launch traced here: 541 us
  Pallas kernels  191 us (35%)
  starting transfers between devices  135 us (25%)
  waiting for transfers between devices  114 us (21%)
  other arithmetic  58.5 us (11%)
  local copies, waits for them, and re-layouts  28.8 us (5%)
  between operations  15.2 us (3%)
    pallas_call x15, Pallas kernels, run(): pl.pallas_call(body, grid=(steps,), in_specs=ins, out_specs=[spec for spe...  191 us
    ppermute x9, starting transfers between devices, send(): lax.ppermute(self.out[0], 'z', [(i, i + 1) for i in range(step)])  40.8 us
    all_gather x2, waiting for transfers between devices, gather(): return lax.all_gather(piece, 'z', axis=0, tiled=True)  28.8 us
    convert_element_type x8, other arithmetic, add_low(): return (left.astype(F32) + right.astype(F32)).astype(BF16)  27.4 us
    ppermute x9, waiting for transfers between devices, send(): lax.ppermute(self.out[0], 'z', [(i, i + 1) for i in range(step)])  26.9 us
    ppermute x6, starting transfers between devices, send(): lax.ppermute(right, 'z', [(i, i + 1) for i in range(step, count - 1)])  25.7 us
    ppermute x20, starting transfers between devices, partner(): lax.ppermute(array, names, [(i, count - 1 - i) for i in range(count)])  23.9 us
    ppermute x20, waiting for transfers between devices, partner(): lax.ppermute(array, names, [(i, count - 1 - i) for i in range(count)])  23.8 us
  transfers between devices with their start and end apart: 62, of which 20 were waited for; matrix products, arithmetic and copies ran while one was open for 14% of the time, Pallas kernels for 35%

commit v1 on v0

--- a/solution.py
+++ b/solution.py
@@ -74,7 +74,7 @@
         out_shape=shapes,
         scratch_shapes=scratch,
         cost_estimate=pl.CostEstimate(
-            flops=flops // 64, bytes_accessed=moved // 64, transcendentals=transcendentals // 64
+            flops=3 * flops, bytes_accessed=moved, transcendentals=transcendentals
         ),
         compiler_params=pltpu.CompilerParams(vmem_limit_bytes=VMEM_BYTES),
     )(*args)

time: 551 us -> 546 us (level)
  no operation moved by 1% of the time
where the time goes in v1:
time: 546 us; the launch traced here: 536 us
  Pallas kernels  190 us (35%)
  starting transfers between devices  132 us (24%)
  waiting for transfers between devices  114 us (21%)
  other arithmetic  55.8 us (10%)
  local copies, waits for them, and re-layouts  28.9 us (5%)
  between operations  15.1 us (3%)
    pallas_call x15, Pallas kernels, run(): pl.pallas_call(body, grid=(steps,), in_specs=ins, out_specs=[spec for spe...  190 us
    ppermute x9, starting transfers between devices, send(): lax.ppermute(self.out[0], 'z', [(i, i + 1) for i in range(step)])  36.5 us
    ppermute x6, starting transfers between devices, send(): lax.ppermute(right, 'z', [(i, i + 1) for i in range(step, count - 1)])  27.6 us
    ppermute x9, waiting for transfers between devices, send(): lax.ppermute(self.out[0], 'z', [(i, i + 1) for i in range(step)])  27.1 us
    convert_element_type x8, other arithmetic, add_low(): return (left.astype(F32) + right.astype(F32)).astype(BF16)  25.1 us
    ppermute x20, starting transfers between devices, partner(): lax.ppermute(array, names, [(i, count - 1 - i) for i in range(count)])  24.7 us
    all_gather x2, waiting for transfers between devices, gather(): return lax.all_gather(piece, 'z', axis=0, tiled=True)  24.1 us
    ppermute x20, waiting for transfers between devices, partner(): lax.ppermute(array, names, [(i, count - 1 - i) for i in range(count)])  22.6 us
  transfers between devices with their start and end apart: 62, of which 20 were waited for; matrix products, arithmetic and copies ran while one was open for 14% of the time, Pallas kernels for 35%

profile of v1, /device:TPU:0, one launch (start us, length us, event | category | flops | bytes accessed | tf_op | source)
XLA Modules:
  0.0 536.0 jit_solution(4883654474253184536)
XLA Ops:
  9.9 5.6 %collective-permute-done.1 = bf16[256,768]{1,0:T(8,128)(2,1)} collective-permute-done((bf16[256,768]{1,0:T(8,128)(2,1)}, bf16[256,768]{1,0:T(8,128)(2,1)}, u32[]{:S(2)}, u32[]{:S(2)}) %collective-permute-start.1) | collective-permute-done | bytes 393248 | tf_op jit(solution)/shard_map/ppermute | solution.py:427
  29.6 5.4 %multiply_sine_fusion = (f32[2048,32]{1,0:T(8,128)S(1)}, f32[2048,32]{1,0:T(8,128)S(1)}, f32[2048,32]{1,0:T(8,128)}) fusion(f32[32]{0:T(128)S(1)} %multiply_power_fusion, f32[2048]{0:T(1024)S(1)} %bitcast.132), kind=kLoop, calls=%fused_computation.43 | loop fusion | flops 131072 | bytes 794752 | tf_op jit(solution)/shard_map/sin | solution.py:28
  34.9 5.4 %collective-permute-done.3 = bf16[64,2048]{1,0:T(8,128)(2,1)S(1)} collective-permute-done((bf16[64,2048]{1,0:T(8,128)(2,1)S(1)}, bf16[64,2048]{1,0:T(8,128)(2,1)S(1)}, u32[]{:S(2)}, u32[]{:S(2)}) %collective-permute-start.3) | collective-permute-done | bytes 262176 | tf_op jit(solution)/shard_map/ppermute | solution.py:476
  42.8 12.0 %collective-permute-start.8 = (bf16[256,1024]{1,0:T(8,128)(2,1)S(1)}, bf16[256,1024]{1,0:T(8,128)(2,1)S(1)}, u32[]{:S(2)}, u32[]{:S(2)}) collective-permute-start(bf16[256,1024]{1,0:T(8,128)(2,1)S(1)} %pad_maximum_fusion.1), channel_id=1, source_target_pairs={{0,1},{1,0},{2,3},{3,2},{4,5},{5,4},{6,7},{7,6},{8,9},{9,8},{10,11... | collective-permute-start | bytes 1572872 | tf_op jit(solution)/shard_map/ppermute | solution.py:427
  57.4 14.5 %shard_map.254 = (bf16[2048,2048]{1,0:T(8,128)(2,1)}, bf16[2048,2048]{1,0:T(8,128)(2,1)}, f32[2048,128]{1,0:T(8,128)}) custom-call(bf16[1024,2048]{1,0:T(8,128)(2,1)} %bitcast.119, bf16[1024,2048]{1,0:T(8,128)(2,1)} %collective-permute-done.other_ref.refs_0_, f32[1,2048]{1,0:T(1,128)} %bitcast.135, f32[1,2048]{1,0:T(1,128)} %bitcast.133, ...), custom_call_target="tpu_custom_call" | custom-call | flops 251658240 | bytes 26247168 | tf_op jit(solution)/shard_map/pallas_call | solution.py:69
  76.5 17.2 %collective-permute-start.9 = (bf16[512,1024]{1,0:T(8,128)(2,1)}, bf16[512,1024]{1,0:T(8,128)(2,1)S(1)}, u32[]{:S(2)}, u32[]{:S(2)}) collective-permute-start(bf16[512,1024]{1,0:T(8,128)(2,1)} %maximum_select_fusion.refs_4_.refs_8_), channel_id=1, source_target_pairs={{0,2},{2,4},{4,6},{1,3},{3,5},{5,7},{8,10},{10,12},{12,14},{9,11},... | collective-permute-start | bytes 3145736 | tf_op jit(solution)/shard_map/ppermute | solution.py:366
  100.2 9.6 %shard_map.255.g_ref.refs_2_.refs_0_ = bf16[2048,2048]{1,0:T(8,128)(2,1)} custom-call(s32[4]{0:T(128)} %pad_add_fusion.1.starts_ref, bf16[1024,512]{1,0:T(8,128)(2,1)} %bitcast.112, bf16[1024,512]{1,0:T(8,128)(2,1)} %copy-done.17, bf16[1024,512]{1,0:T(8,128)(2,1)} %collective-permute-done.5.refs_2_, bf16[1024,512]{1,0:T(8,128)(2,1)} %copy-done.18, ...), custom_call_target="tpu_custom_call" | custom-call | flops 12582912 | bytes 16777232 | tf_op jit(solution)/shard_map/pallas_call | solution.py:69
  109.8 24.1 %all-gather.5.cloned.1.call-done.dense_ref.refs_1_ = bf16[256,2048]{1,0:T(8,128)(2,1)} async-done(((bf16[64,2048]{1,0:T(8,128)(2,1)}), bf16[256,2048]{1,0:T(8,128)(2,1)}) %all-gather.5.cloned.1.call-update) | async-done | bytes 1048592 | tf_op jit(solution)/shard_map/all_gather | solution.py:448
  135.9 24.1 %shard_map.256 = (bf16[2048,256]{1,0:T(8,128)(2,1)}, bf16[2048,768]{1,0:T(8,128)(2,1)}, f32[1,768]{1,0:T(1,128)}) custom-call(bf16[2048,2048]{1,0:T(8,128)(2,1)} %get-tuple-element.211.normed_ref.refs_0_, bf16[2048,768]{1,0:T(8,128)(2,1)} %all-gather.3.cloned.1.call-done.joined_ref.refs_3_, f32[1,768]{1,0:T(1,128)} %reshape.166.bias_ref, ...), custom_call_target="tpu_custom_call" | custom-call | flops 37044092928 | bytes 28334080 | tf_op jit(solution)/shard_map/pallas_call | solution.py:69
  160.1 4.9 collective-permute-done.16.refs_6_.refs_10_
  167.1 14.4 %shard_map.257 = bf16[4,2,256,1024]{3,2,1,0:T(8,128)(2,1)} custom-call(bf16[2048,2048]{1,0:T(8,128)(2,1)} %get-tuple-element.211.normed_ref.refs_0_, bf16[2048,768]{1,0:T(8,128)(2,1)} %get-tuple-element.290.refs_1_.refs_2_, bf16[2048,2048]{1,0:T(8,128)(2,1)} %shard_map.255.g_ref.refs_2_.refs_0_, bf16[2048,256]{1,0:T(8,128)(2,1)} %get-tuple-element.270.refs_3_.refs_0_), custom_call_target="tpu_custom_call" | custom-call | flops 25769803776 | bytes 25165824 | tf_op jit(solution)/shard_map/pallas_call | solution.py:69
  184.1 6.5 %collective-permute-start.21 = (bf16[2,256,1024]{2,1,0:T(8,128)(2,1)S(1)}, bf16[2,256,1024]{2,1,0:T(8,128)(2,1)}, u32[]{:S(2)}, u32[]{:S(2)}) collective-permute-start(bf16[2,256,1024]{2,1,0:T(8,128)(2,1)S(1)} %get-tuple-element.363), channel_id=1, source_target_pairs={{0,2},{1,3},{8,10},{9,11},{16,18},{17,19},{24,26},{25,27}} | collective-permute-start | bytes 3145736 | tf_op jit(solution)/shard_map/ppermute | solution.py:339
  192.3 5.5 %collective-permute-start.19 = (bf16[256,2048]{1,0:T(8,128)(2,1)S(1)}, bf16[256,2048]{1,0:T(8,128)(2,1)}, u32[]{:S(2)}, u32[]{:S(2)}) collective-permute-start(bf16[256,2048]{1,0:T(8,128)(2,1)S(1)} %copy-done.21), channel_id=1, source_target_pairs={{0,2},{2,4},{4,6},{1,3},{3,5},{5,7},{8,10},{10,12},{12,14},{9,11},... | collective-permute-start | bytes 3145736 | tf_op jit(solution)/shard_map/ppermute | solution.py:366
  197.9 17.5 %shard_map.258 = (bf16[2048,1024]{1,0:T(8,128)(2,1)}, bf16[2048,1024]{1,0:T(8,128)(2,1)}) custom-call(s32[1]{0:T(128)} %bitcast.1.index_ref, bf16[2048,2048]{1,0:T(8,128)(2,1)} %get-tuple-element.275.refs_0_, bf16[512,1024]{1,0:T(8,128)(2,1)} %copy-done.37, bf16[512,1024]{1,0:T(8,128)(2,1)} %copy-done.35, bf16[512,1024]{1,0:T(8,128)(2,1)} %copy-done.34, ...), custom_call_target="tpu_custom_call" | custom-call | flops 25769803776 | bytes 24121348 | tf_op jit(solution)/shard_map/pallas_call | solution.py:69
  215.4 13.4 %shard_map.259 = bf16[4,2,256,1024]{3,2,1,0:T(8,128)(2,1)} custom-call(bf16[2048,2048]{1,0:T(8,128)(2,1)} %shard_map.255.g_ref.refs_2_.refs_0_, bf16[2048,1024]{1,0:T(8,128)(2,1)} %get-tuple-element.264.refs_1_.refs_2_), custom_call_target="tpu_custom_call" | custom-call | flops 25769803776 | bytes 16777216 | tf_op jit(solution)/shard_map/pallas_call | solution.py:69
  232.7 5.5 %collective-permute-start.25 = (bf16[2,256,1024]{2,1,0:T(8,128)(2,1)S(1)}, bf16[2,256,1024]{2,1,0:T(8,128)(2,1)}, u32[]{:S(2)}, u32[]{:S(2)}) collective-permute-start(bf16[2,256,1024]{2,1,0:T(8,128)(2,1)S(1)} %get-tuple-element.230), channel_id=1, source_target_pairs={{0,2},{1,3},{8,10},{9,11},{16,18},{17,19},{24,26},{25,27}} | collective-permute-start | bytes 3145736 | tf_op jit(solution)/shard_map/ppermute | solution.py:339
  247.8 9.1 %collective-permute-done.25 = bf16[2,256,1024]{2,1,0:T(8,128)(2,1)} collective-permute-done((bf16[2,256,1024]{2,1,0:T(8,128)(2,1)S(1)}, bf16[2,256,1024]{2,1,0:T(8,128)(2,1)}, u32[]{:S(2)}, u32[]{:S(2)}) %collective-permute-start.25) | collective-permute-done | bytes 1048608 | tf_op jit(solution)/shard_map/ppermute | solution.py:339
  256.9 8.7 %collective-permute-done.24.refs_6_.refs_8_ = bf16[256,2048]{1,0:T(8,128)(2,1)} collective-permute-done((bf16[256,2048]{1,0:T(8,128)(2,1)}, bf16[256,2048]{1,0:T(8,128)(2,1)}, u32[]{:S(2)}, u32[]{:S(2)}) %collective-permute-start.24) | collective-permute-done | bytes 1048608 | tf_op jit(solution)/shard_map/ppermute | solution.py:367
  272.4 4.7 fusion.17
  277.1 10.7 %collective-permute-done.29 = bf16[2,256,1024]{2,1,0:T(8,128)(2,1)S(1)} collective-permute-done((bf16[2,256,1024]{2,1,0:T(8,128)(2,1)}, bf16[2,256,1024]{2,1,0:T(8,128)(2,1)S(1)}, u32[]{:S(2)}, u32[]{:S(2)}) %collective-permute-start.29) | collective-permute-done | bytes 1048608 | tf_op jit(solution)/shard_map/ppermute | solution.py:339
  287.9 6.6 %collective-permute-done.28.refs_7_.refs_9_ = bf16[256,2048]{1,0:T(8,128)(2,1)} collective-permute-done((bf16[256,2048]{1,0:T(8,128)(2,1)}, bf16[256,2048]{1,0:T(8,128)(2,1)}, u32[]{:S(2)}, u32[]{:S(2)}) %collective-permute-start.28) | collective-permute-done | bytes 1048608 | tf_op jit(solution)/shard_map/ppermute | solution.py:367
  296.8 4.8 collective-permute-start.31
  301.6 15.2 %shard_map.260 = (bf16[2048,1024]{1,0:T(8,128)(2,1)}, f32[1,1024]{1,0:T(1,128)}) custom-call(s32[1]{0:T(128)} %bitcast.1.index_ref, bf16[2048,2048]{1,0:T(8,128)(2,1)} %shard_map.255.g_ref.refs_2_.refs_0_, bf16[256,2048]{1,0:T(8,128)(2,1)} %collective-permute-done.27.refs_1_.refs_3_, bf16[256,2048]{1,0:T(8,128)(2,1)} %collective-permute-done.23.refs_2_.refs_4_, ...), custom_call_target="tpu_custom_call" | custom-call | flops 25769803776 | bytes 24121348 | tf_op jit(solution)/shard_map/pallas_call | solution.py:69
  316.8 11.0 %shard_map.261 = bf16[1,4,1024,512]{3,2,1,0:T(8,128)(2,1)} custom-call(s32[1]{0:T(128)} %bitcast.1.index_ref, bf16[2048,256]{1,0:T(8,128)(2,1)} %get-tuple-element.270.refs_3_.refs_0_, bf16[256,2048]{1,0:T(8,128)(2,1)} %all-gather.5.cloned.1.call-done.dense_ref.refs_1_, bf16[2048,1024]{1,0:T(8,128)(2,1)} %get-tuple-element.264.refs_1_.refs_2_, ...), custom_call_target="tpu_custom_call" | custom-call | flops 16106127360 | bytes 17825796 | tf_op jit(solution)/shard_map/pallas_call | solution.py:69
  339.4 13.4 %shard_map.263 = bf16[4,2,256,1024]{3,2,1,0:T(8,128)(2,1)} custom-call(bf16[2048,2048]{1,0:T(8,128)(2,1)} %get-tuple-element.275.refs_0_, bf16[2048,1024]{1,0:T(8,128)(2,1)} %get-tuple-element.289.refs_1_.refs_4_), custom_call_target="tpu_custom_call" | custom-call | flops 25769803776 | bytes 16777216 | tf_op jit(solution)/shard_map/pallas_call | solution.py:69
  354.6 11.6 %shard_map.262 = bf16[1,4,1024,512]{3,2,1,0:T(8,128)(2,1)} custom-call(s32[1]{0:T(128)} %bitcast.1.index_ref, bf16[2048,256]{1,0:T(8,128)(2,1)} %get-tuple-element.270.refs_3_.refs_0_, bf16[256,2048]{1,0:T(8,128)(2,1)} %all-gather.5.cloned.1.call-done.dense_ref.refs_1_, bf16[2048,1024]{1,0:T(8,128)(2,1)} %get-tuple-element.264.refs_1_.refs_2_, ...), custom_call_target="tpu_custom_call" | custom-call | flops 16106127360 | bytes 22020100 | tf_op jit(solution)/shard_map/pallas_call | solution.py:69
  370.3 18.6 %shard_map.264 = (bf16[2,4,512,512]{3,2,1,0:T(8,128)(2,1)}, f32[4,2048]{1,0:T(4,128)}) custom-call(s32[1]{0:T(128)} %bitcast.1.index_ref, bf16[1024,2048]{1,0:T(8,128)(2,1)} %collective-permute-done.other_ref.refs_0_, f32[2048,128]{1,0:T(8,128)} %get-tuple-element.279.refs_1_, bf16[2048,768]{1,0:T(8,128)(2,1)} %get-tuple-element.290.refs_1_.refs_2_, ...), custom_call_target="tpu_custom_call" | custom-call | flops 22548578304 | bytes 27312132 | tf_op jit(solution)/shard_map/pallas_call | solution.py:69
  403.2 18.8 %shard_map.265 = (bf16[2,4,512,512]{3,2,1,0:T(8,128)(2,1)}, f32[4,2048]{1,0:T(4,128)}) custom-call(s32[1]{0:T(128)} %bitcast.1.index_ref, bf16[1024,2048]{1,0:T(8,128)(2,1)} %bitcast.120, f32[2048,128]{1,0:T(8,128)} %get-tuple-element.279.refs_1_, bf16[2048,768]{1,0:T(8,128)(2,1)} %get-tuple-element.290.refs_1_.refs_2_, ...), custom_call_target="tpu_custom_call" | custom-call | flops 22548578304 | bytes 31506436 | tf_op jit(solution)/shard_map/pallas_call | solution.py:69
  428.3 4.6 collective-permute-start.43
  467.3 4.9 fusion.7
  484.9 9.5 %collective-permute-done.46 = bf16[512,512]{1,0:T(8,128)(2,1)S(1)} collective-permute-done((bf16[512,512]{1,0:T(8,128)(2,1)S(1)}, bf16[512,512]{1,0:T(8,128)(2,1)S(1)}, u32[]{:S(2)}, u32[]{:S(2)}) %collective-permute-start.46) | collective-permute-done | bytes 524320 | tf_op jit(solution)/shard_map/ppermute | solution.py:427
  498.1 5.1 collective-permute-done.54
  (261 shorter events, 178.1 us)
Async XLA Ops:
  7.2 102.6 %all-gather.3.cloned.1.call-start = ((), (), s32[]{:S(2)}) async-start(), calls=%async_computation.4 | async-start | bytes 3932160 | tf_op jit(solution)/shard_map/all_gather | solution.py:448
  7.3 34.0 %collective-permute-start = (bf16[1024,2048]{1,0:T(8,128)(2,1)}, bf16[1024,2048]{1,0:T(8,128)(2,1)}, u32[]{:S(2)}, u32[]{:S(2)}) collective-permute-start(bf16[1024,2048]{1,0:T(8,128)(2,1)} %bitcast.118), channel_id=1, source_target_pairs={{0,1},{1,0},{2,3},{3,2},{4,5},{5,4},{6,7},{7,6},{8,9},{9,8},{10,11... | collective-permute-start | bytes 12582920 | tf_op jit(solution)/shard_map/ppermute | solution.py:427
  17.7 116.1 %all-gather.5.cloned.1.call-start = ((), (), s32[]{:S(2)}) async-start(), calls=%async_computation.5 | async-start | bytes 1310720 | tf_op jit(solution)/shard_map/all_gather | solution.py:448
  17.8 55.5 %collective-permute-start.7 = (bf16[1024,512]{1,0:T(8,128)(2,1)S(1)}, bf16[1024,512]{1,0:T(8,128)(2,1)}, u32[]{:S(2)}, u32[]{:S(2)}) collective-permute-start(bf16[1024,512]{1,0:T(8,128)(2,1)S(1)} %bitcast.113), channel_id=1, source_target_pairs={{0,24},{8,16},{16,8},{24,0},{1,25},{9,17},{17,9},{25,1},{2,26},{10... | collective-permute-start | bytes 3145736 | tf_op jit(solution)/shard_map/ppermute | solution.py:427
  21.7 51.6 %collective-permute-start.6 = (bf16[1024,512]{1,0:T(8,128)(2,1)S(1)}, bf16[1024,512]{1,0:T(8,128)(2,1)}, u32[]{:S(2)}, u32[]{:S(2)}) collective-permute-start(bf16[1024,512]{1,0:T(8,128)(2,1)S(1)} %bitcast.114), channel_id=1, source_target_pairs={{0,16},{16,0},{1,17},{17,1},{2,18},{18,2},{3,19},{19,3},{4,20},{20... | collective-permute-start | bytes 3145736 | tf_op jit(solution)/shard_map/ppermute | solution.py:427
  40.3 33.0 %collective-permute-start.5 = (bf16[1024,512]{1,0:T(8,128)(2,1)S(1)}, bf16[1024,512]{1,0:T(8,128)(2,1)}, u32[]{:S(2)}, u32[]{:S(2)}) collective-permute-start(bf16[1024,512]{1,0:T(8,128)(2,1)S(1)} %bitcast.115), channel_id=1, source_target_pairs={{0,8},{8,0},{1,9},{9,1},{2,10},{10,2},{3,11},{11,3},{4,12},{12,4},... | collective-permute-start | bytes 3145736 | tf_op jit(solution)/shard_map/ppermute | solution.py:427
  42.8 29.1 %collective-permute-start.8 = (bf16[256,1024]{1,0:T(8,128)(2,1)S(1)}, bf16[256,1024]{1,0:T(8,128)(2,1)S(1)}, u32[]{:S(2)}, u32[]{:S(2)}) collective-permute-start(bf16[256,1024]{1,0:T(8,128)(2,1)S(1)} %pad_maximum_fusion.1), channel_id=1, source_target_pairs={{0,1},{1,0},{2,3},{3,2},{4,5},{5,4},{6,7},{7,6},{8,9},{9,8},{10,11... | collective-permute-start | bytes 1572872 | tf_op jit(solution)/shard_map/ppermute | solution.py:427
  74.5 59.4 %collective-permute-start.10 = (bf16[512,1024]{1,0:T(8,128)(2,1)}, bf16[512,1024]{1,0:T(8,128)(2,1)}, u32[]{:S(2)}, u32[]{:S(2)}) collective-permute-start(bf16[512,1024]{1,0:T(8,128)(2,1)} %maximum_select_fusion.refs_4_.refs_8_), channel_id=1, source_target_pairs={{2,0},{4,2},{6,4},{3,1},{5,3},{7,5},{10,8},{12,10},{14,12},{11,9},... | collective-permute-start | bytes 3145736 | tf_op jit(solution)/shard_map/ppermute | solution.py:367
  76.5 57.4 %collective-permute-start.9 = (bf16[512,1024]{1,0:T(8,128)(2,1)}, bf16[512,1024]{1,0:T(8,128)(2,1)S(1)}, u32[]{:S(2)}, u32[]{:S(2)}) collective-permute-start(bf16[512,1024]{1,0:T(8,128)(2,1)} %maximum_select_fusion.refs_4_.refs_8_), channel_id=1, source_target_pairs={{0,2},{2,4},{4,6},{1,3},{3,5},{5,7},{8,10},{10,12},{12,14},{9,11},... | collective-permute-start | bytes 3145736 | tf_op jit(solution)/shard_map/ppermute | solution.py:366
  133.9 26.2 %collective-permute-start.15 = (bf16[512,1024]{1,0:T(8,128)(2,1)S(1)}, bf16[512,1024]{1,0:T(8,128)(2,1)S(1)}, u32[]{:S(2)}, u32[]{:S(2)}) collective-permute-start(bf16[512,1024]{1,0:T(8,128)(2,1)S(1)} %collective-permute-done.9.refs_3_.refs_7_), channel_id=1, source_target_pairs={{2,4},{4,6},{3,5},{5,7},{10,12},{12,14},{11,13},{13,15},{18,20},{2... | collective-permute-start | bytes 3145736 | tf_op jit(solution)/shard_map/ppermute | solution.py:366
  134.6 30.3 %collective-permute-start.16 = (bf16[512,1024]{1,0:T(8,128)(2,1)}, bf16[512,1024]{1,0:T(8,128)(2,1)S(1)}, u32[]{:S(2)}, u32[]{:S(2)}) collective-permute-start(bf16[512,1024]{1,0:T(8,128)(2,1)} %collective-permute-done.10.refs_5_.refs_9_), channel_id=1, source_target_pairs={{2,0},{4,2},{3,1},{5,3},{10,8},{12,10},{11,9},{13,11},{18,16},{20,... | collective-permute-start | bytes 3145736 | tf_op jit(solution)/shard_map/ppermute | solution.py:367
  183.3 47.4 %collective-permute-start.22 = (bf16[2,256,1024]{2,1,0:T(8,128)(2,1)S(1)}, bf16[2,256,1024]{2,1,0:T(8,128)(2,1)S(1)}, u32[]{:S(2)}, u32[]{:S(2)}) collective-permute-start(bf16[2,256,1024]{2,1,0:T(8,128)(2,1)S(1)} %get-tuple-element.362), channel_id=1, source_target_pairs={{6,4},{7,5},{14,12},{15,13},{22,20},{23,21},{30,28},{31,29}} | collective-permute-start | bytes 3145736 | tf_op jit(solution)/shard_map/ppermute | solution.py:340
  184.1 46.7 %collective-permute-start.21 = (bf16[2,256,1024]{2,1,0:T(8,128)(2,1)S(1)}, bf16[2,256,1024]{2,1,0:T(8,128)(2,1)}, u32[]{:S(2)}, u32[]{:S(2)}) collective-permute-start(bf16[2,256,1024]{2,1,0:T(8,128)(2,1)S(1)} %get-tuple-element.363), channel_id=1, source_target_pairs={{0,2},{1,3},{8,10},{9,11},{16,18},{17,19},{24,26},{25,27}} | collective-permute-start | bytes 3145736 | tf_op jit(solution)/shard_map/ppermute | solution.py:339
  191.1 39.7 %collective-permute-start.20 = (bf16[256,2048]{1,0:T(8,128)(2,1)S(1)}, bf16[256,2048]{1,0:T(8,128)(2,1)}, u32[]{:S(2)}, u32[]{:S(2)}) collective-permute-start(bf16[256,2048]{1,0:T(8,128)(2,1)S(1)} %copy-done.21), channel_id=1, source_target_pairs={{2,0},{4,2},{6,4},{3,1},{5,3},{7,5},{10,8},{12,10},{14,12},{11,9},... | collective-permute-start | bytes 3145736 | tf_op jit(solution)/shard_map/ppermute | solution.py:367
  192.3 40.3 %collective-permute-start.19 = (bf16[256,2048]{1,0:T(8,128)(2,1)S(1)}, bf16[256,2048]{1,0:T(8,128)(2,1)}, u32[]{:S(2)}, u32[]{:S(2)}) collective-permute-start(bf16[256,2048]{1,0:T(8,128)(2,1)S(1)} %copy-done.21), channel_id=1, source_target_pairs={{0,2},{2,4},{4,6},{1,3},{3,5},{5,7},{8,10},{10,12},{12,14},{9,11},... | collective-permute-start | bytes 3145736 | tf_op jit(solution)/shard_map/ppermute | solution.py:366
  295.5 32.3 %collective-permute-start.32 = (bf16[2,256,1024]{2,1,0:T(8,128)(2,1)S(1)}, bf16[2,256,1024]{2,1,0:T(8,128)(2,1)S(1)}, u32[]{:S(2)}, u32[]{:S(2)}) collective-permute-start(bf16[2,256,1024]{2,1,0:T(8,128)(2,1)S(1)} %get-tuple-element.354), channel_id=1, source_target_pairs={{6,4},{4,2},{2,0},{7,5},{5,3},{3,1},{14,12},{12,10},{10,8},{15,13}... | collective-permute-start | bytes 3145736 | tf_op jit(solution)/shard_map/ppermute | solution.py:340
  296.8 31.1 %collective-permute-start.31 = (bf16[2,256,1024]{2,1,0:T(8,128)(2,1)S(1)}, bf16[2,256,1024]{2,1,0:T(8,128)(2,1)S(1)}, u32[]{:S(2)}, u32[]{:S(2)}) collective-permute-start(bf16[2,256,1024]{2,1,0:T(8,128)(2,1)S(1)} %get-tuple-element.355), channel_id=1, source_target_pairs={{0,2},{2,4},{4,6},{1,3},{3,5},{5,7},{8,10},{10,12},{12,14},{9,11},... | collective-permute-start | bytes 3145736 | tf_op jit(solution)/shard_map/ppermute | solution.py:339
  327.8 26.8 %collective-permute-start.33 = (bf16[1,4,1024,512]{3,2,1,0:T(8,128)(2,1)}, bf16[1,4,1024,512]{3,2,1,0:T(8,128)(2,1)}, u32[]{:S(2)}, u32[]{:S(2)}) collective-permute-start(bf16[1,4,1024,512]{3,2,1,0:T(8,128)(2,1)} %shard_map.261), channel_id=1, source_target_pairs={{0,1},{1,0},{2,3},{3,2},{4,5},{5,4},{6,7},{7,6},{8,9},{9,8},{10,11... | collective-permute-start | bytes 12582920 | tf_op jit(solution)/shard_map/ppermute | solution.py:427
  330.7 35.5 %all-to-all-start = ((bf16[4,128,1024]{2,1,0:T(8,128)(2,1)}), bf16[4,128,1024]{2,1,0:T(8,128)(2,1)S(1)}, u32[]{:S(2)}, u32[]{:S(2)}) async-start(bf16[4,128,1024]{2,1,0:T(8,128)(2,1)} %bitcast.24), calls=%async_computation | async-start | bytes 2097152 | tf_op jit(solution)/shard_map/all_to_all | solution.py:630
  334.9 90.2 %reduce-scatter.4.cloned.1.call-start = ((), (), s32[]{:S(2)}) async-start(), calls=%async_computation.6 | async-start | bytes 5242880
  334.9 31.4 %collective-permute-start.34 = (bf16[2,256,1024]{2,1,0:T(8,128)(2,1)}, bf16[2,256,1024]{2,1,0:T(8,128)(2,1)}, u32[]{:S(2)}, u32[]{:S(2)}) collective-permute-start(bf16[2,256,1024]{2,1,0:T(8,128)(2,1)} %get-tuple-element.273), channel_id=1, source_target_pairs={{0,2},{2,4},{1,3},{3,5},{8,10},{10,12},{9,11},{11,13},{16,18},{18,... | collective-permute-start | bytes 3145736 | tf_op jit(solution)/shard_map/ppermute | solution.py:339
  337.7 28.6 %collective-permute-start.35 = (bf16[2,256,1024]{2,1,0:T(8,128)(2,1)}, bf16[2,256,1024]{2,1,0:T(8,128)(2,1)}, u32[]{:S(2)}, u32[]{:S(2)}) collective-permute-start(bf16[2,256,1024]{2,1,0:T(8,128)(2,1)} %get-tuple-element.274), channel_id=1, source_target_pairs={{6,4},{4,2},{7,5},{5,3},{14,12},{12,10},{15,13},{13,11},{22,20},{2... | collective-permute-start | bytes 3145736 | tf_op jit(solution)/shard_map/ppermute | solution.py:340
  393.7 28.3 %collective-permute-start.39 = (bf16[2,256,1024]{2,1,0:T(8,128)(2,1)}, bf16[2,256,1024]{2,1,0:T(8,128)(2,1)S(1)}, u32[]{:S(2)}, u32[]{:S(2)}) collective-permute-start(bf16[2,256,1024]{2,1,0:T(8,128)(2,1)} %get-tuple-element.298), channel_id=1, source_target_pairs={{0,2},{2,4},{4,6},{1,3},{3,5},{5,7},{8,10},{10,12},{12,14},{9,11},... | collective-permute-start | bytes 3145736 | tf_op jit(solution)/shard_map/ppermute | solution.py:339
  397.1 28.0 %collective-permute-start.40 = (bf16[2,256,1024]{2,1,0:T(8,128)(2,1)}, bf16[2,256,1024]{2,1,0:T(8,128)(2,1)S(1)}, u32[]{:S(2)}, u32[]{:S(2)}) collective-permute-start(bf16[2,256,1024]{2,1,0:T(8,128)(2,1)} %get-tuple-element.299), channel_id=1, source_target_pairs={{6,4},{4,2},{2,0},{7,5},{5,3},{3,1},{14,12},{12,10},{10,8},{15,13}... | collective-permute-start | bytes 3145736 | tf_op jit(solution)/shard_map/ppermute | solution.py:340
  428.3 27.5 %collective-permute-start.43 = (bf16[2,256,1024]{2,1,0:T(8,128)(2,1)}, bf16[2,256,1024]{2,1,0:T(8,128)(2,1)}, u32[]{:S(2)}, u32[]{:S(2)}) collective-permute-start(bf16[2,256,1024]{2,1,0:T(8,128)(2,1)} %get-tuple-element.308), channel_id=1, source_target_pairs={{0,2},{2,4},{1,3},{3,5},{8,10},{10,12},{9,11},{11,13},{16,18},{18,... | collective-permute-start | bytes 3145736 | tf_op jit(solution)/shard_map/ppermute | solution.py:339
  438.1 26.4 %collective-permute-start.41 = (bf16[2,512,512]{2,1,0:T(8,128)(2,1)}, bf16[2,512,512]{2,1,0:T(8,128)(2,1)}, u32[]{:S(2)}, u32[]{:S(2)}) collective-permute-start(bf16[2,512,512]{2,1,0:T(8,128)(2,1)} %dynamic-slice_bitcast_fusion.1), channel_id=1, source_target_pairs={{0,16},{16,0},{1,17},{17,1},{2,18},{18,2},{3,19},{19,3},{4,20},{20... | collective-permute-start | bytes 3145736 | tf_op jit(solution)/shard_map/ppermute | solution.py:427
  439.2 28.1 %collective-permute-start.42 = (bf16[2,512,512]{2,1,0:T(8,128)(2,1)}, bf16[2,512,512]{2,1,0:T(8,128)(2,1)S(1)}, u32[]{:S(2)}, u32[]{:S(2)}) collective-permute-start(bf16[2,512,512]{2,1,0:T(8,128)(2,1)} %dynamic-slice_bitcast_fusion), channel_id=1, source_target_pairs={{0,8},{8,0},{1,9},{9,1},{2,10},{10,2},{3,11},{11,3},{4,12},{12,4},... | collective-permute-start | bytes 3145736 | tf_op jit(solution)/shard_map/ppermute | solution.py:427
  444.2 40.7 %all-to-all-start.1 = ((bf16[4,128,1024]{2,1,0:T(8,128)(2,1)}), bf16[4,128,1024]{2,1,0:T(8,128)(2,1)S(1)}, u32[]{:S(2)}, u32[]{:S(2)}) async-start(bf16[4,128,1024]{2,1,0:T(8,128)(2,1)} %bitcast.42), calls=%async_computation.1 | async-start | bytes 2097152 | tf_op jit(solution)/shard_map/all_to_all | solution.py:630
  450.5 29.8 %collective-permute-start.52 = (f32[24576]{0:T(1024)S(1)}, f32[24576]{0:T(1024)S(1)}, u32[]{:S(2)}, u32[]{:S(2)}) collective-permute-start(f32[24576]{0:T(1024)S(1)} %add_add_fusion.1), channel_id=1, source_target_pairs={{0,10},{2,8},{4,14},{6,12},{8,2},{10,0},{12,6},{14,4},{1,11},{3,9}... | collective-permute-start | bytes 294920 | tf_op jit(solution)/shard_map/ppermute | solution.py:874
  455.8 26.3 %collective-permute-start.51 = (f32[24576]{0:T(1024)S(1)}, f32[24576]{0:T(1024)S(1)}, u32[]{:S(2)}, u32[]{:S(2)}) collective-permute-start(f32[24576]{0:T(1024)S(1)} %add_add_fusion.1), channel_id=1, source_target_pairs={{0,8},{2,10},{4,12},{6,14},{8,0},{10,2},{12,4},{14,6},{1,9},{3,11}... | collective-permute-start | bytes 294920 | tf_op jit(solution)/shard_map/ppermute | solution.py:874
  456.2 26.1 %collective-permute-start.50 = (f32[24576]{0:T(1024)S(1)}, f32[24576]{0:T(1024)S(1)}, u32[]{:S(2)}, u32[]{:S(2)}) collective-permute-start(f32[24576]{0:T(1024)S(1)} %add_add_fusion.1), channel_id=1, source_target_pairs={{0,2},{2,0},{4,6},{6,4},{1,3},{3,1},{5,7},{7,5},{8,10},{10,8},{12,... | collective-permute-start | bytes 294920 | tf_op jit(solution)/shard_map/ppermute | solution.py:872
  475.7 27.5 %collective-permute-start.54 = (bf16[2,256,1024]{2,1,0:T(8,128)(2,1)}, bf16[2,256,1024]{2,1,0:T(8,128)(2,1)}, u32[]{:S(2)}, u32[]{:S(2)}) collective-permute-start(bf16[2,256,1024]{2,1,0:T(8,128)(2,1)} %get-tuple-element.330), channel_id=1, source_target_pairs={{6,4},{4,2},{2,0},{7,5},{5,3},{3,1},{14,12},{12,10},{10,8},{15,13}... | collective-permute-start | bytes 3145736 | tf_op jit(solution)/shard_map/ppermute | solution.py:340
  (68 other events, 907.5 us)
Sparse Core Ops, SparseCore 0:
  17.8 70.5 all-gather.2
  90.6 43.1 all-gather.4
  366.4 51.1 reduce-scatter.3

commit v2 on v1

--- a/solution.py
+++ b/solution.py
@@ -74,7 +74,7 @@
         out_shape=shapes,
         scratch_shapes=scratch,
         cost_estimate=pl.CostEstimate(
-            flops=3 * flops, bytes_accessed=moved, transcendentals=transcendentals
+            flops=2 * flops, bytes_accessed=moved, transcendentals=transcendentals
         ),
         compiler_params=pltpu.CompilerParams(vmem_limit_bytes=VMEM_BYTES),
     )(*args)

time: 546 us -> 545 us (level)
  transfers between devices with their start and end apart: 62 -> 62, of which waited for: 20 -> 21; matrix products, arithmetic and copies ran while one was open for 14% -> 15% of each run, Pallas kernels for 35% -> 35%
where the time goes in v2:
time: 545 us; the launch traced here: 535 us
  Pallas kernels  190 us (35%)
  starting transfers between devices  128 us (23%)
  waiting for transfers between devices  112 us (21%)
  other arithmetic  59.6 us (11%)
  local copies, waits for them, and re-layouts  30.9 us (6%)
  between operations  15 us (3%)
    pallas_call x15, Pallas kernels, run(): pl.pallas_call(body, grid=(steps,), in_specs=ins, out_specs=[spec for spe...  190 us
    ppermute x9, starting transfers between devices, send(): lax.ppermute(self.out[0], 'z', [(i, i + 1) for i in range(step)])  35.6 us
    ppermute x6, starting transfers between devices, send(): lax.ppermute(right, 'z', [(i, i + 1) for i in range(step, count - 1)])  27.6 us
    convert_element_type x8, other arithmetic, add_low(): return (left.astype(F32) + right.astype(F32)).astype(BF16)  27 us
    ppermute x9, waiting for transfers between devices, send(): lax.ppermute(self.out[0], 'z', [(i, i + 1) for i in range(step)])  25.1 us
    all_gather x2, waiting for transfers between devices, gather(): return lax.all_gather(piece, 'z', axis=0, tiled=True)  24.1 us
    ppermute x20, waiting for transfers between devices, partner(): lax.ppermute(array, names, [(i, count - 1 - i) for i in range(count)])  23.9 us
    ppermute x20, starting transfers between devices, partner(): lax.ppermute(array, names, [(i, count - 1 - i) for i in range(count)])  23.8 us
  transfers between devices with their start and end apart: 62, of which 21 were waited for; matrix products, arithmetic and copies ran while one was open for 15% of the time, Pallas kernels for 35%

profile of v2, /device:TPU:0, one launch (start us, length us, event | category | flops | bytes accessed | tf_op | source)
XLA Modules:
  0.0 535.3 jit_solution(8601116010138561232)
XLA Ops:
  9.9 5.6 %collective-permute-done.1 = bf16[256,768]{1,0:T(8,128)(2,1)} collective-permute-done((bf16[256,768]{1,0:T(8,128)(2,1)}, bf16[256,768]{1,0:T(8,128)(2,1)}, u32[]{:S(2)}, u32[]{:S(2)}) %collective-permute-start.1) | collective-permute-done | bytes 393248 | tf_op jit(solution)/shard_map/ppermute | solution.py:427
  29.6 5.4 %multiply_sine_fusion = (f32[2048,32]{1,0:T(8,128)S(1)}, f32[2048,32]{1,0:T(8,128)S(1)}, f32[2048,32]{1,0:T(8,128)}) fusion(f32[32]{0:T(128)S(1)} %multiply_power_fusion, f32[2048]{0:T(1024)S(1)} %bitcast.132), kind=kLoop, calls=%fused_computation.43 | loop fusion | flops 131072 | bytes 794752 | tf_op jit(solution)/shard_map/sin | solution.py:28
  34.9 5.3 collective-permute-done.3
  42.8 12.0 %collective-permute-start.8 = (bf16[256,1024]{1,0:T(8,128)(2,1)S(1)}, bf16[256,1024]{1,0:T(8,128)(2,1)S(1)}, u32[]{:S(2)}, u32[]{:S(2)}) collective-permute-start(bf16[256,1024]{1,0:T(8,128)(2,1)S(1)} %pad_maximum_fusion.1), channel_id=1, source_target_pairs={{0,1},{1,0},{2,3},{3,2},{4,5},{5,4},{6,7},{7,6},{8,9},{9,8},{10,11... | collective-permute-start | bytes 1572872 | tf_op jit(solution)/shard_map/ppermute | solution.py:427
  57.4 14.5 %shard_map.254 = (bf16[2048,2048]{1,0:T(8,128)(2,1)}, bf16[2048,2048]{1,0:T(8,128)(2,1)}, f32[2048,128]{1,0:T(8,128)}) custom-call(bf16[1024,2048]{1,0:T(8,128)(2,1)} %bitcast.119, bf16[1024,2048]{1,0:T(8,128)(2,1)} %collective-permute-done.other_ref.refs_0_, f32[1,2048]{1,0:T(1,128)} %bitcast.135, f32[1,2048]{1,0:T(1,128)} %bitcast.133, ...), custom_call_target="tpu_custom_call" | custom-call | flops 167772160 | bytes 26247168 | tf_op jit(solution)/shard_map/pallas_call | solution.py:69
  76.5 17.3 %collective-permute-start.9 = (bf16[512,1024]{1,0:T(8,128)(2,1)}, bf16[512,1024]{1,0:T(8,128)(2,1)S(1)}, u32[]{:S(2)}, u32[]{:S(2)}) collective-permute-start(bf16[512,1024]{1,0:T(8,128)(2,1)} %maximum_select_fusion.refs_4_.refs_8_), channel_id=1, source_target_pairs={{0,2},{2,4},{4,6},{1,3},{3,5},{5,7},{8,10},{10,12},{12,14},{9,11},... | collective-permute-start | bytes 3145736 | tf_op jit(solution)/shard_map/ppermute | solution.py:366
  100.2 9.6 %shard_map.255.g_ref.refs_2_.refs_0_ = bf16[2048,2048]{1,0:T(8,128)(2,1)} custom-call(s32[4]{0:T(128)} %pad_add_fusion.1.starts_ref, bf16[1024,512]{1,0:T(8,128)(2,1)} %bitcast.112, bf16[1024,512]{1,0:T(8,128)(2,1)} %copy-done.13, bf16[1024,512]{1,0:T(8,128)(2,1)} %collective-permute-done.5.refs_2_, bf16[1024,512]{1,0:T(8,128)(2,1)} %copy-done.14, ...), custom_call_target="tpu_custom_call" | custom-call | flops 8388608 | bytes 16777232 | tf_op jit(solution)/shard_map/pallas_call | solution.py:69
  109.8 24.1 %all-gather.5.cloned.1.call-done.dense_ref.refs_1_ = bf16[256,2048]{1,0:T(8,128)(2,1)} async-done(((bf16[64,2048]{1,0:T(8,128)(2,1)}), bf16[256,2048]{1,0:T(8,128)(2,1)}) %all-gather.5.cloned.1.call-update) | async-done | bytes 1048592 | tf_op jit(solution)/shard_map/all_gather | solution.py:448
  136.0 24.1 %shard_map.256 = (bf16[2048,256]{1,0:T(8,128)(2,1)}, bf16[2048,768]{1,0:T(8,128)(2,1)}, f32[1,768]{1,0:T(1,128)}) custom-call(bf16[2048,2048]{1,0:T(8,128)(2,1)} %get-tuple-element.211.normed_ref.refs_0_, bf16[2048,768]{1,0:T(8,128)(2,1)} %all-gather.3.cloned.1.call-done.joined_ref.refs_3_, f32[1,768]{1,0:T(1,128)} %reshape.166.bias_ref, ...), custom_call_target="tpu_custom_call" | custom-call | flops 24696061952 | bytes 28334080 | tf_op jit(solution)/shard_map/pallas_call | solution.py:69
  160.1 4.9 collective-permute-done.16.refs_6_.refs_10_
  167.2 14.4 %shard_map.257 = bf16[4,2,256,1024]{3,2,1,0:T(8,128)(2,1)} custom-call(bf16[2048,2048]{1,0:T(8,128)(2,1)} %get-tuple-element.211.normed_ref.refs_0_, bf16[2048,768]{1,0:T(8,128)(2,1)} %get-tuple-element.290.refs_1_.refs_2_, bf16[2048,2048]{1,0:T(8,128)(2,1)} %shard_map.255.g_ref.refs_2_.refs_0_, bf16[2048,256]{1,0:T(8,128)(2,1)} %get-tuple-element.270.refs_3_.refs_0_), custom_call_target="tpu_custom_call" | custom-call | flops 17179869184 | bytes 25165824 | tf_op jit(solution)/shard_map/pallas_call | solution.py:69
  184.1 6.5 %collective-permute-start.21 = (bf16[2,256,1024]{2,1,0:T(8,128)(2,1)S(1)}, bf16[2,256,1024]{2,1,0:T(8,128)(2,1)}, u32[]{:S(2)}, u32[]{:S(2)}) collective-permute-start(bf16[2,256,1024]{2,1,0:T(8,128)(2,1)S(1)} %get-tuple-element.363), channel_id=1, source_target_pairs={{0,2},{1,3},{8,10},{9,11},{16,18},{17,19},{24,26},{25,27}} | collective-permute-start | bytes 3145736 | tf_op jit(solution)/shard_map/ppermute | solution.py:339
  192.4 5.5 %collective-permute-start.19 = (bf16[256,2048]{1,0:T(8,128)(2,1)S(1)}, bf16[256,2048]{1,0:T(8,128)(2,1)}, u32[]{:S(2)}, u32[]{:S(2)}) collective-permute-start(bf16[256,2048]{1,0:T(8,128)(2,1)S(1)} %copy-done.15), channel_id=1, source_target_pairs={{0,2},{2,4},{4,6},{1,3},{3,5},{5,7},{8,10},{10,12},{12,14},{9,11},... | collective-permute-start | bytes 3145736 | tf_op jit(solution)/shard_map/ppermute | solution.py:366
  197.9 17.5 %shard_map.258 = (bf16[2048,1024]{1,0:T(8,128)(2,1)}, bf16[2048,1024]{1,0:T(8,128)(2,1)}) custom-call(s32[1]{0:T(128)} %bitcast.1.index_ref, bf16[2048,2048]{1,0:T(8,128)(2,1)} %get-tuple-element.275.refs_0_, bf16[512,1024]{1,0:T(8,128)(2,1)} %copy-done.27, bf16[512,1024]{1,0:T(8,128)(2,1)} %copy-done.25, bf16[512,1024]{1,0:T(8,128)(2,1)} %copy-done.24, ...), custom_call_target="tpu_custom_call" | custom-call | flops 17179869184 | bytes 24121348 | tf_op jit(solution)/shard_map/pallas_call | solution.py:69
  215.5 13.4 %shard_map.259 = bf16[4,2,256,1024]{3,2,1,0:T(8,128)(2,1)} custom-call(bf16[2048,2048]{1,0:T(8,128)(2,1)} %shard_map.255.g_ref.refs_2_.refs_0_, bf16[2048,1024]{1,0:T(8,128)(2,1)} %get-tuple-element.264.refs_1_.refs_2_), custom_call_target="tpu_custom_call" | custom-call | flops 17179869184 | bytes 16777216 | tf_op jit(solution)/shard_map/pallas_call | solution.py:69
  232.7 5.5 %collective-permute-start.25 = (bf16[2,256,1024]{2,1,0:T(8,128)(2,1)S(1)}, bf16[2,256,1024]{2,1,0:T(8,128)(2,1)}, u32[]{:S(2)}, u32[]{:S(2)}) collective-permute-start(bf16[2,256,1024]{2,1,0:T(8,128)(2,1)S(1)} %get-tuple-element.230), channel_id=1, source_target_pairs={{0,2},{1,3},{8,10},{9,11},{16,18},{17,19},{24,26},{25,27}} | collective-permute-start | bytes 3145736 | tf_op jit(solution)/shard_map/ppermute | solution.py:339
  248.2 8.7 %collective-permute-done.25 = bf16[2,256,1024]{2,1,0:T(8,128)(2,1)} collective-permute-done((bf16[2,256,1024]{2,1,0:T(8,128)(2,1)S(1)}, bf16[2,256,1024]{2,1,0:T(8,128)(2,1)}, u32[]{:S(2)}, u32[]{:S(2)}) %collective-permute-start.25) | collective-permute-done | bytes 1048608 | tf_op jit(solution)/shard_map/ppermute | solution.py:339
  256.9 8.7 %collective-permute-done.24.refs_6_.refs_8_ = bf16[256,2048]{1,0:T(8,128)(2,1)} collective-permute-done((bf16[256,2048]{1,0:T(8,128)(2,1)}, bf16[256,2048]{1,0:T(8,128)(2,1)}, u32[]{:S(2)}, u32[]{:S(2)}) %collective-permute-start.24) | collective-permute-done | bytes 1048608 | tf_op jit(solution)/shard_map/ppermute | solution.py:367
  272.5 4.7 fusion.17
  277.2 10.8 %collective-permute-done.29 = bf16[2,256,1024]{2,1,0:T(8,128)(2,1)S(1)} collective-permute-done((bf16[2,256,1024]{2,1,0:T(8,128)(2,1)}, bf16[2,256,1024]{2,1,0:T(8,128)(2,1)S(1)}, u32[]{:S(2)}, u32[]{:S(2)}) %collective-permute-start.29) | collective-permute-done | bytes 1048608 | tf_op jit(solution)/shard_map/ppermute | solution.py:339
  288.0 6.6 %collective-permute-done.28.refs_7_.refs_9_ = bf16[256,2048]{1,0:T(8,128)(2,1)} collective-permute-done((bf16[256,2048]{1,0:T(8,128)(2,1)}, bf16[256,2048]{1,0:T(8,128)(2,1)}, u32[]{:S(2)}, u32[]{:S(2)}) %collective-permute-start.28) | collective-permute-done | bytes 1048608 | tf_op jit(solution)/shard_map/ppermute | solution.py:367
  296.9 4.8 collective-permute-start.31
  301.7 15.2 %shard_map.260 = (bf16[2048,1024]{1,0:T(8,128)(2,1)}, f32[1,1024]{1,0:T(1,128)}) custom-call(s32[1]{0:T(128)} %bitcast.1.index_ref, bf16[2048,2048]{1,0:T(8,128)(2,1)} %shard_map.255.g_ref.refs_2_.refs_0_, bf16[256,2048]{1,0:T(8,128)(2,1)} %collective-permute-done.27.refs_1_.refs_3_, bf16[256,2048]{1,0:T(8,128)(2,1)} %collective-permute-done.23.refs_2_.refs_4_, ...), custom_call_target="tpu_custom_call" | custom-call | flops 17179869184 | bytes 24121348 | tf_op jit(solution)/shard_map/pallas_call | solution.py:69
  316.9 11.0 %shard_map.261 = bf16[1,4,1024,512]{3,2,1,0:T(8,128)(2,1)} custom-call(s32[1]{0:T(128)} %bitcast.1.index_ref, bf16[2048,256]{1,0:T(8,128)(2,1)} %get-tuple-element.270.refs_3_.refs_0_, bf16[256,2048]{1,0:T(8,128)(2,1)} %all-gather.5.cloned.1.call-done.dense_ref.refs_1_, bf16[2048,1024]{1,0:T(8,128)(2,1)} %get-tuple-element.264.refs_1_.refs_2_, ...), custom_call_target="tpu_custom_call" | custom-call | flops 10737418240 | bytes 17825796 | tf_op jit(solution)/shard_map/pallas_call | solution.py:69
  339.4 13.4 %shard_map.263 = bf16[4,2,256,1024]{3,2,1,0:T(8,128)(2,1)} custom-call(bf16[2048,2048]{1,0:T(8,128)(2,1)} %get-tuple-element.275.refs_0_, bf16[2048,1024]{1,0:T(8,128)(2,1)} %get-tuple-element.289.refs_1_.refs_4_), custom_call_target="tpu_custom_call" | custom-call | flops 17179869184 | bytes 16777216 | tf_op jit(solution)/shard_map/pallas_call | solution.py:69
  355.6 11.6 %shard_map.262 = bf16[1,4,1024,512]{3,2,1,0:T(8,128)(2,1)} custom-call(s32[1]{0:T(128)} %bitcast.1.index_ref, bf16[2048,256]{1,0:T(8,128)(2,1)} %get-tuple-element.270.refs_3_.refs_0_, bf16[256,2048]{1,0:T(8,128)(2,1)} %all-gather.5.cloned.1.call-done.dense_ref.refs_1_, bf16[2048,1024]{1,0:T(8,128)(2,1)} %get-tuple-element.264.refs_1_.refs_2_, ...), custom_call_target="tpu_custom_call" | custom-call | flops 10737418240 | bytes 22020100 | tf_op jit(solution)/shard_map/pallas_call | solution.py:69
  374.9 17.9 %shard_map.264 = (bf16[2,4,512,512]{3,2,1,0:T(8,128)(2,1)}, f32[4,2048]{1,0:T(4,128)}) custom-call(s32[1]{0:T(128)} %bitcast.1.index_ref, bf16[1024,2048]{1,0:T(8,128)(2,1)} %collective-permute-done.other_ref.refs_0_, f32[2048,128]{1,0:T(8,128)} %get-tuple-element.279.refs_1_, bf16[2048,768]{1,0:T(8,128)(2,1)} %get-tuple-element.290.refs_1_.refs_2_, ...), custom_call_target="tpu_custom_call" | custom-call | flops 15032385536 | bytes 27312132 | tf_op jit(solution)/shard_map/pallas_call | solution.py:69
  405.3 18.8 %shard_map.265 = (bf16[2,4,512,512]{3,2,1,0:T(8,128)(2,1)}, f32[4,2048]{1,0:T(4,128)}) custom-call(s32[1]{0:T(128)} %bitcast.1.index_ref, bf16[1024,2048]{1,0:T(8,128)(2,1)} %bitcast.120, f32[2048,128]{1,0:T(8,128)} %get-tuple-element.279.refs_1_, bf16[2048,768]{1,0:T(8,128)(2,1)} %get-tuple-element.290.refs_1_.refs_2_, ...), custom_call_target="tpu_custom_call" | custom-call | flops 15032385536 | bytes 31506436 | tf_op jit(solution)/shard_map/pallas_call | solution.py:69
  460.3 4.7 collective-permute-done.41
  468.2 4.6 fusion.7
  486.3 9.7 %collective-permute-done.46 = bf16[512,512]{1,0:T(8,128)(2,1)} collective-permute-done((bf16[512,512]{1,0:T(8,128)(2,1)}, bf16[512,512]{1,0:T(8,128)(2,1)}, u32[]{:S(2)}, u32[]{:S(2)}) %collective-permute-start.46) | collective-permute-done | bytes 524320 | tf_op jit(solution)/shard_map/ppermute | solution.py:427
  497.5 5.1 collective-permute-done.54
  (241 shorter events, 178.4 us)
Async XLA Ops:
  7.2 102.6 %all-gather.3.cloned.1.call-start = ((), (), s32[]{:S(2)}) async-start(), calls=%async_computation.4 | async-start | bytes 3932160 | tf_op jit(solution)/shard_map/all_gather | solution.py:448
  7.3 34.0 %collective-permute-start = (bf16[1024,2048]{1,0:T(8,128)(2,1)}, bf16[1024,2048]{1,0:T(8,128)(2,1)}, u32[]{:S(2)}, u32[]{:S(2)}) collective-permute-start(bf16[1024,2048]{1,0:T(8,128)(2,1)} %bitcast.118), channel_id=1, source_target_pairs={{0,1},{1,0},{2,3},{3,2},{4,5},{5,4},{6,7},{7,6},{8,9},{9,8},{10,11... | collective-permute-start | bytes 12582920 | tf_op jit(solution)/shard_map/ppermute | solution.py:427
  17.7 116.2 %all-gather.5.cloned.1.call-start = ((), (), s32[]{:S(2)}) async-start(), calls=%async_computation.5 | async-start | bytes 1310720 | tf_op jit(solution)/shard_map/all_gather | solution.py:448
  17.8 55.6 %collective-permute-start.7 = (bf16[1024,512]{1,0:T(8,128)(2,1)S(1)}, bf16[1024,512]{1,0:T(8,128)(2,1)}, u32[]{:S(2)}, u32[]{:S(2)}) collective-permute-start(bf16[1024,512]{1,0:T(8,128)(2,1)S(1)} %bitcast.113), channel_id=1, source_target_pairs={{0,24},{8,16},{16,8},{24,0},{1,25},{9,17},{17,9},{25,1},{2,26},{10... | collective-permute-start | bytes 3145736 | tf_op jit(solution)/shard_map/ppermute | solution.py:427
  21.7 51.7 %collective-permute-start.6 = (bf16[1024,512]{1,0:T(8,128)(2,1)S(1)}, bf16[1024,512]{1,0:T(8,128)(2,1)}, u32[]{:S(2)}, u32[]{:S(2)}) collective-permute-start(bf16[1024,512]{1,0:T(8,128)(2,1)S(1)} %bitcast.114), channel_id=1, source_target_pairs={{0,16},{16,0},{1,17},{17,1},{2,18},{18,2},{3,19},{19,3},{4,20},{20... | collective-permute-start | bytes 3145736 | tf_op jit(solution)/shard_map/ppermute | solution.py:427
  40.3 33.1 %collective-permute-start.5 = (bf16[1024,512]{1,0:T(8,128)(2,1)S(1)}, bf16[1024,512]{1,0:T(8,128)(2,1)}, u32[]{:S(2)}, u32[]{:S(2)}) collective-permute-start(bf16[1024,512]{1,0:T(8,128)(2,1)S(1)} %bitcast.115), channel_id=1, source_target_pairs={{0,8},{8,0},{1,9},{9,1},{2,10},{10,2},{3,11},{11,3},{4,12},{12,4},... | collective-permute-start | bytes 3145736 | tf_op jit(solution)/shard_map/ppermute | solution.py:427
  42.8 29.1 %collective-permute-start.8 = (bf16[256,1024]{1,0:T(8,128)(2,1)S(1)}, bf16[256,1024]{1,0:T(8,128)(2,1)S(1)}, u32[]{:S(2)}, u32[]{:S(2)}) collective-permute-start(bf16[256,1024]{1,0:T(8,128)(2,1)S(1)} %pad_maximum_fusion.1), channel_id=1, source_target_pairs={{0,1},{1,0},{2,3},{3,2},{4,5},{5,4},{6,7},{7,6},{8,9},{9,8},{10,11... | collective-permute-start | bytes 1572872 | tf_op jit(solution)/shard_map/ppermute | solution.py:427
  74.5 59.4 %collective-permute-start.10 = (bf16[512,1024]{1,0:T(8,128)(2,1)}, bf16[512,1024]{1,0:T(8,128)(2,1)}, u32[]{:S(2)}, u32[]{:S(2)}) collective-permute-start(bf16[512,1024]{1,0:T(8,128)(2,1)} %maximum_select_fusion.refs_4_.refs_8_), channel_id=1, source_target_pairs={{2,0},{4,2},{6,4},{3,1},{5,3},{7,5},{10,8},{12,10},{14,12},{11,9},... | collective-permute-start | bytes 3145736 | tf_op jit(solution)/shard_map/ppermute | solution.py:367
  76.5 57.4 %collective-permute-start.9 = (bf16[512,1024]{1,0:T(8,128)(2,1)}, bf16[512,1024]{1,0:T(8,128)(2,1)S(1)}, u32[]{:S(2)}, u32[]{:S(2)}) collective-permute-start(bf16[512,1024]{1,0:T(8,128)(2,1)} %maximum_select_fusion.refs_4_.refs_8_), channel_id=1, source_target_pairs={{0,2},{2,4},{4,6},{1,3},{3,5},{5,7},{8,10},{10,12},{12,14},{9,11},... | collective-permute-start | bytes 3145736 | tf_op jit(solution)/shard_map/ppermute | solution.py:366
  133.9 26.2 %collective-permute-start.15 = (bf16[512,1024]{1,0:T(8,128)(2,1)S(1)}, bf16[512,1024]{1,0:T(8,128)(2,1)S(1)}, u32[]{:S(2)}, u32[]{:S(2)}) collective-permute-start(bf16[512,1024]{1,0:T(8,128)(2,1)S(1)} %collective-permute-done.9.refs_3_.refs_7_), channel_id=1, source_target_pairs={{2,4},{4,6},{3,5},{5,7},{10,12},{12,14},{11,13},{13,15},{18,20},{2... | collective-permute-start | bytes 3145736 | tf_op jit(solution)/shard_map/ppermute | solution.py:366
  134.7 30.3 %collective-permute-start.16 = (bf16[512,1024]{1,0:T(8,128)(2,1)}, bf16[512,1024]{1,0:T(8,128)(2,1)S(1)}, u32[]{:S(2)}, u32[]{:S(2)}) collective-permute-start(bf16[512,1024]{1,0:T(8,128)(2,1)} %collective-permute-done.10.refs_5_.refs_9_), channel_id=1, source_target_pairs={{2,0},{4,2},{3,1},{5,3},{10,8},{12,10},{11,9},{13,11},{18,16},{20,... | collective-permute-start | bytes 3145736 | tf_op jit(solution)/shard_map/ppermute | solution.py:367
  183.4 47.4 %collective-permute-start.22 = (bf16[2,256,1024]{2,1,0:T(8,128)(2,1)S(1)}, bf16[2,256,1024]{2,1,0:T(8,128)(2,1)S(1)}, u32[]{:S(2)}, u32[]{:S(2)}) collective-permute-start(bf16[2,256,1024]{2,1,0:T(8,128)(2,1)S(1)} %get-tuple-element.362), channel_id=1, source_target_pairs={{6,4},{7,5},{14,12},{15,13},{22,20},{23,21},{30,28},{31,29}} | collective-permute-start | bytes 3145736 | tf_op jit(solution)/shard_map/ppermute | solution.py:340
  184.1 46.7 %collective-permute-start.21 = (bf16[2,256,1024]{2,1,0:T(8,128)(2,1)S(1)}, bf16[2,256,1024]{2,1,0:T(8,128)(2,1)}, u32[]{:S(2)}, u32[]{:S(2)}) collective-permute-start(bf16[2,256,1024]{2,1,0:T(8,128)(2,1)S(1)} %get-tuple-element.363), channel_id=1, source_target_pairs={{0,2},{1,3},{8,10},{9,11},{16,18},{17,19},{24,26},{25,27}} | collective-permute-start | bytes 3145736 | tf_op jit(solution)/shard_map/ppermute | solution.py:339
  191.1 39.7 %collective-permute-start.20 = (bf16[256,2048]{1,0:T(8,128)(2,1)S(1)}, bf16[256,2048]{1,0:T(8,128)(2,1)}, u32[]{:S(2)}, u32[]{:S(2)}) collective-permute-start(bf16[256,2048]{1,0:T(8,128)(2,1)S(1)} %copy-done.15), channel_id=1, source_target_pairs={{2,0},{4,2},{6,4},{3,1},{5,3},{7,5},{10,8},{12,10},{14,12},{11,9},... | collective-permute-start | bytes 3145736 | tf_op jit(solution)/shard_map/ppermute | solution.py:367
  192.4 40.3 %collective-permute-start.19 = (bf16[256,2048]{1,0:T(8,128)(2,1)S(1)}, bf16[256,2048]{1,0:T(8,128)(2,1)}, u32[]{:S(2)}, u32[]{:S(2)}) collective-permute-start(bf16[256,2048]{1,0:T(8,128)(2,1)S(1)} %copy-done.15), channel_id=1, source_target_pairs={{0,2},{2,4},{4,6},{1,3},{3,5},{5,7},{8,10},{10,12},{12,14},{9,11},... | collective-permute-start | bytes 3145736 | tf_op jit(solution)/shard_map/ppermute | solution.py:366
  295.6 32.3 %collective-permute-start.32 = (bf16[2,256,1024]{2,1,0:T(8,128)(2,1)S(1)}, bf16[2,256,1024]{2,1,0:T(8,128)(2,1)S(1)}, u32[]{:S(2)}, u32[]{:S(2)}) collective-permute-start(bf16[2,256,1024]{2,1,0:T(8,128)(2,1)S(1)} %get-tuple-element.354), channel_id=1, source_target_pairs={{6,4},{4,2},{2,0},{7,5},{5,3},{3,1},{14,12},{12,10},{10,8},{15,13}... | collective-permute-start | bytes 3145736 | tf_op jit(solution)/shard_map/ppermute | solution.py:340
  296.9 31.0 %collective-permute-start.31 = (bf16[2,256,1024]{2,1,0:T(8,128)(2,1)S(1)}, bf16[2,256,1024]{2,1,0:T(8,128)(2,1)S(1)}, u32[]{:S(2)}, u32[]{:S(2)}) collective-permute-start(bf16[2,256,1024]{2,1,0:T(8,128)(2,1)S(1)} %get-tuple-element.355), channel_id=1, source_target_pairs={{0,2},{2,4},{4,6},{1,3},{3,5},{5,7},{8,10},{10,12},{12,14},{9,11},... | collective-permute-start | bytes 3145736 | tf_op jit(solution)/shard_map/ppermute | solution.py:339
  327.9 27.7 %collective-permute-start.33 = (bf16[1,4,1024,512]{3,2,1,0:T(8,128)(2,1)}, bf16[1,4,1024,512]{3,2,1,0:T(8,128)(2,1)}, u32[]{:S(2)}, u32[]{:S(2)}) collective-permute-start(bf16[1,4,1024,512]{3,2,1,0:T(8,128)(2,1)} %shard_map.261), channel_id=1, source_target_pairs={{0,1},{1,0},{2,3},{3,2},{4,5},{5,4},{6,7},{7,6},{8,9},{9,8},{10,11... | collective-permute-start | bytes 12582920 | tf_op jit(solution)/shard_map/ppermute | solution.py:427
  330.8 36.4 %all-to-all-start = ((bf16[4,128,1024]{2,1,0:T(8,128)(2,1)}), bf16[4,128,1024]{2,1,0:T(8,128)(2,1)S(1)}, u32[]{:S(2)}, u32[]{:S(2)}) async-start(bf16[4,128,1024]{2,1,0:T(8,128)(2,1)} %bitcast.24), calls=%async_computation | async-start | bytes 2097152 | tf_op jit(solution)/shard_map/all_to_all | solution.py:630
  334.9 91.0 %reduce-scatter.4.cloned.1.call-start = ((), (), s32[]{:S(2)}) async-start(), calls=%async_computation.6 | async-start | bytes 5242880
  334.9 32.3 %collective-permute-start.34 = (bf16[2,256,1024]{2,1,0:T(8,128)(2,1)}, bf16[2,256,1024]{2,1,0:T(8,128)(2,1)}, u32[]{:S(2)}, u32[]{:S(2)}) collective-permute-start(bf16[2,256,1024]{2,1,0:T(8,128)(2,1)} %get-tuple-element.273), channel_id=1, source_target_pairs={{0,2},{2,4},{1,3},{3,5},{8,10},{10,12},{9,11},{11,13},{16,18},{18,... | collective-permute-start | bytes 3145736 | tf_op jit(solution)/shard_map/ppermute | solution.py:339
  337.8 29.5 %collective-permute-start.35 = (bf16[2,256,1024]{2,1,0:T(8,128)(2,1)}, bf16[2,256,1024]{2,1,0:T(8,128)(2,1)}, u32[]{:S(2)}, u32[]{:S(2)}) collective-permute-start(bf16[2,256,1024]{2,1,0:T(8,128)(2,1)} %get-tuple-element.274), channel_id=1, source_target_pairs={{6,4},{4,2},{7,5},{5,3},{14,12},{12,10},{15,13},{13,11},{22,20},{2... | collective-permute-start | bytes 3145736 | tf_op jit(solution)/shard_map/ppermute | solution.py:340
  394.9 29.2 %collective-permute-start.39 = (bf16[2,256,1024]{2,1,0:T(8,128)(2,1)}, bf16[2,256,1024]{2,1,0:T(8,128)(2,1)S(1)}, u32[]{:S(2)}, u32[]{:S(2)}) collective-permute-start(bf16[2,256,1024]{2,1,0:T(8,128)(2,1)} %get-tuple-element.298), channel_id=1, source_target_pairs={{0,2},{2,4},{4,6},{1,3},{3,5},{5,7},{8,10},{10,12},{12,14},{9,11},... | collective-permute-start | bytes 3145736 | tf_op jit(solution)/shard_map/ppermute | solution.py:339
  399.2 26.7 %collective-permute-start.40 = (bf16[2,256,1024]{2,1,0:T(8,128)(2,1)}, bf16[2,256,1024]{2,1,0:T(8,128)(2,1)S(1)}, u32[]{:S(2)}, u32[]{:S(2)}) collective-permute-start(bf16[2,256,1024]{2,1,0:T(8,128)(2,1)} %get-tuple-element.299), channel_id=1, source_target_pairs={{6,4},{4,2},{2,0},{7,5},{5,3},{3,1},{14,12},{12,10},{10,8},{15,13}... | collective-permute-start | bytes 3145736 | tf_op jit(solution)/shard_map/ppermute | solution.py:340
  429.1 27.2 %collective-permute-start.43 = (bf16[2,256,1024]{2,1,0:T(8,128)(2,1)}, bf16[2,256,1024]{2,1,0:T(8,128)(2,1)}, u32[]{:S(2)}, u32[]{:S(2)}) collective-permute-start(bf16[2,256,1024]{2,1,0:T(8,128)(2,1)} %get-tuple-element.308), channel_id=1, source_target_pairs={{0,2},{2,4},{1,3},{3,5},{8,10},{10,12},{9,11},{11,13},{16,18},{18,... | collective-permute-start | bytes 3145736 | tf_op jit(solution)/shard_map/ppermute | solution.py:339
  438.6 26.4 %collective-permute-start.41 = (bf16[2,512,512]{2,1,0:T(8,128)(2,1)}, bf16[2,512,512]{2,1,0:T(8,128)(2,1)}, u32[]{:S(2)}, u32[]{:S(2)}) collective-permute-start(bf16[2,512,512]{2,1,0:T(8,128)(2,1)} %dynamic-slice_bitcast_fusion.1), channel_id=1, source_target_pairs={{0,16},{16,0},{1,17},{17,1},{2,18},{18,2},{3,19},{19,3},{4,20},{20... | collective-permute-start | bytes 3145736 | tf_op jit(solution)/shard_map/ppermute | solution.py:427
  439.8 28.4 %collective-permute-start.42 = (bf16[2,512,512]{2,1,0:T(8,128)(2,1)}, bf16[2,512,512]{2,1,0:T(8,128)(2,1)}, u32[]{:S(2)}, u32[]{:S(2)}) collective-permute-start(bf16[2,512,512]{2,1,0:T(8,128)(2,1)} %dynamic-slice_bitcast_fusion), channel_id=1, source_target_pairs={{0,8},{8,0},{1,9},{9,1},{2,10},{10,2},{3,11},{11,3},{4,12},{12,4},... | collective-permute-start | bytes 3145736 | tf_op jit(solution)/shard_map/ppermute | solution.py:427
  444.5 41.7 %all-to-all-start.1 = ((bf16[4,128,1024]{2,1,0:T(8,128)(2,1)}), bf16[4,128,1024]{2,1,0:T(8,128)(2,1)S(1)}, u32[]{:S(2)}, u32[]{:S(2)}) async-start(bf16[4,128,1024]{2,1,0:T(8,128)(2,1)} %bitcast.42), calls=%async_computation.1 | async-start | bytes 2097152 | tf_op jit(solution)/shard_map/all_to_all | solution.py:630
  451.7 30.4 %collective-permute-start.52 = (f32[24576]{0:T(1024)S(1)}, f32[24576]{0:T(1024)S(1)}, u32[]{:S(2)}, u32[]{:S(2)}) collective-permute-start(f32[24576]{0:T(1024)S(1)} %add_add_fusion.1), channel_id=1, source_target_pairs={{0,10},{2,8},{4,14},{6,12},{8,2},{10,0},{12,6},{14,4},{1,11},{3,9}... | collective-permute-start | bytes 294920 | tf_op jit(solution)/shard_map/ppermute | solution.py:874
  456.3 26.9 %collective-permute-start.51 = (f32[24576]{0:T(1024)S(1)}, f32[24576]{0:T(1024)S(1)}, u32[]{:S(2)}, u32[]{:S(2)}) collective-permute-start(f32[24576]{0:T(1024)S(1)} %add_add_fusion.1), channel_id=1, source_target_pairs={{0,8},{2,10},{4,12},{6,14},{8,0},{10,2},{12,4},{14,6},{1,9},{3,11}... | collective-permute-start | bytes 294920 | tf_op jit(solution)/shard_map/ppermute | solution.py:874
  456.4 27.4 %collective-permute-start.50 = (f32[24576]{0:T(1024)S(1)}, f32[24576]{0:T(1024)S(1)}, u32[]{:S(2)}, u32[]{:S(2)}) collective-permute-start(f32[24576]{0:T(1024)S(1)} %add_add_fusion.1), channel_id=1, source_target_pairs={{0,2},{2,0},{4,6},{6,4},{1,3},{3,1},{5,7},{7,5},{8,10},{10,8},{12,... | collective-permute-start | bytes 294920 | tf_op jit(solution)/shard_map/ppermute | solution.py:872
  475.6 27.0 %collective-permute-start.54 = (bf16[2,256,1024]{2,1,0:T(8,128)(2,1)}, bf16[2,256,1024]{2,1,0:T(8,128)(2,1)}, u32[]{:S(2)}, u32[]{:S(2)}) collective-permute-start(bf16[2,256,1024]{2,1,0:T(8,128)(2,1)} %get-tuple-element.330), channel_id=1, source_target_pairs={{6,4},{4,2},{2,0},{7,5},{5,3},{3,1},{14,12},{12,10},{10,8},{15,13}... | collective-permute-start | bytes 3145736 | tf_op jit(solution)/shard_map/ppermute | solution.py:340
  (58 other events, 849.6 us)
Sparse Core Ops, SparseCore 0:
  17.9 70.5 all-gather.2
  90.6 43.2 all-gather.4
  367.4 51.2 reduce-scatter.3
